TPU v7x, 32 devices: a whole 2x2x4 slice. The times are simulated.
32 devices in a mesh: rows: 16 (over z, y, x), vars: 2 (over core).
Axes of the slice: x: 2, y: 2, z: 4, core: 2. Of those that a mesh axis runs over, the one named last changes fastest.
Arguments:
- fields: bfloat16 [16, 65536], P('vars', 'rows'), may hold values from -6 to 6
- stencil: int32 [32768, 4], P('rows'), may hold values from 0 to 1023
- stencil_weight: float32 [32768, 4], P('rows'), may hold values from 0.1 to 1
- owner_map: int32 [2048, 1], P('rows'), may hold values from 0 to 15; in each aligned block of 128 rows (0 to 127, 128 to 255, ...) at most 16 rows name the same one
- embed_weight: bfloat16 [16, 16, 1024], P('vars'), may hold values from -1.5 to 1.5
- embed_bias: bfloat16 [16, 1024], P('vars'), may hold values from -3 to 3
- agg_query: float32 [16, 64], replicated, may hold values from -40 to 40
- out_grad: bfloat16 [4096, 1024], P('rows'), may hold values from -6 to 6
Outputs:
- tokens: bfloat16 [4096, 1024], P('rows', 'vars')
- field_grad: float32 [16, 65536], P('vars', 'rows')
- weight_grad: float32 [16, 16, 1024], P('vars')
- bias_grad: float32 [16, 1024], P('vars')
- query_grad: float32 [16, 64], replicated
Inputs may be any that keep to these rules, and one draw needn't show every extreme that they name: `stencil`: the index of a point within the pixel's own block. `owner_map`: among the 128 patches of one device along rows, no owner is named more than 16 times, a bound that some block reaches.
All inputs are finite; a program needn't handle non-finite values.
Results may differ from a plain program's by a relative error of at most 0.0055.
The roundings to bfloat16 on the way count: a program that leaves them out, or rounds other values in their place, can miss the bound.
Values may be sent and summed in bfloat16 or wider, within the bound.
A program may use at most 128 MiB of HBM per device.

v0:
```python
import math

import jax
import jax.numpy as jnp
from jax import lax
from jax.sharding import PartitionSpec as P

D = 1024
H = 16
DH = 64
P_SIZE = 16
K = 4
PTS_BLK = 1024
PB = 32


def combined_all(value, axis, join):
    pieces = jax.tree.map(lambda part: lax.all_gather(part, axis), value)
    head = jax.tree.map(lambda part: part[0], pieces)
    tail = jax.tree.map(lambda part: part[1:], pieces)
    so_far, _ = lax.scan(lambda so_far, piece: (join(so_far, piece), None), head, tail)
    return so_far


def interp_matrix(index_rows, weight_rows):
    columns = jnp.arange(PTS_BLK, dtype=jnp.int32)
    summed = jnp.zeros((index_rows.shape[0], PTS_BLK), jnp.float32)
    for entry in range(K):
        summed = summed + jnp.where(
            index_rows[:, entry : entry + 1] == columns[None, :],
            weight_rows[:, entry : entry + 1],
            0.0,
        )
    return summed.astype(jnp.bfloat16)


def local(
    fields, stencil, stencil_weight, owner_map, embed_weight, embed_bias, agg_query, out_grad
):
    high = lax.Precision.HIGHEST
    row_devices = lax.axis_size("rows")
    var_devices = lax.axis_size("vars")
    var_local = fields.shape[0]
    point_count = fields.shape[1]
    blocks = point_count // PTS_BLK
    patch_count = owner_map.shape[0]
    capacity = out_grad.shape[0]
    slot_depth = capacity // row_devices
    block_pixels = PB * P_SIZE
    score_scale = 1.0 / math.sqrt(DH)
    field_blocks = fields.reshape(var_local, blocks, PTS_BLK).transpose(1, 0, 2)
    index_blocks = stencil.reshape(blocks, block_pixels, K)
    weight_blocks = stencil_weight.reshape(blocks, block_pixels, K)

    def forward_block(pieces):
        field_block, index_rows, weight_rows = pieces
        matrix = interp_matrix(index_rows, weight_rows)
        return jnp.dot(field_block, matrix.T, preferred_element_type=jnp.float32).astype(
            jnp.bfloat16
        )

    pixels = lax.map(forward_block, (field_blocks, index_blocks, weight_blocks))
    pixels = (
        pixels.reshape(blocks, var_local, PB, P_SIZE)
        .transpose(0, 2, 1, 3)
        .reshape(patch_count, var_local * P_SIZE)
    )
    routes = owner_map[:, 0]
    onehot = (routes[:, None] == jnp.arange(row_devices, dtype=jnp.int32)[None, :]).astype(
        jnp.int32
    )
    order_rank = jnp.sum(onehot * (jnp.cumsum(onehot, axis=0) - 1), axis=1)
    target = routes * slot_depth + order_rank
    outbox = jnp.zeros((capacity, var_local * P_SIZE), jnp.bfloat16).at[target].set(pixels)
    markers = (
        jnp.zeros((capacity,), jnp.bfloat16).at[target].set(jnp.ones((patch_count,), jnp.bfloat16))
    )
    inbox, filled = (
        lax.all_to_all(
            outbox.reshape(row_devices, slot_depth, var_local * P_SIZE),
            "rows",
            split_axis=0,
            concat_axis=0,
            tiled=True,
        ),
        lax.all_to_all(
            markers.reshape(row_devices, slot_depth),
            "rows",
            split_axis=0,
            concat_axis=0,
            tiled=True,
        ),
    )
    filled = filled.reshape(capacity).astype(jnp.float32)
    row_block = min(256, capacity)
    block_count = capacity // row_block
    pix_split = inbox.reshape(block_count, row_block, var_local, P_SIZE)
    bias_f = embed_bias.astype(jnp.float32)

    def embed_rows(pix_rows):
        projected = jnp.einsum(
            "svp,vpd->svd", pix_rows, embed_weight, preferred_element_type=jnp.float32
        )
        return (projected + bias_f[None]).astype(jnp.bfloat16)

    def head_scores(embedded):
        head_view = embedded.astype(jnp.float32).reshape(row_block, var_local, H, DH)
        return (
            head_view,
            jnp.einsum("svhe,he->shv", head_view, agg_query, precision=high) * score_scale,
        )

    def forward_rows(pix_rows):
        embedded = embed_rows(pix_rows)
        head_view, scores = head_scores(embedded)
        peak = jnp.max(scores, axis=2)
        weights_exp = jnp.exp(scores - peak[:, :, None])
        weighted = jnp.einsum("shv,svhe->she", weights_exp, head_view, precision=high)
        return (embedded, peak, jnp.sum(weights_exp, axis=2), weighted)

    embeds, peaks, totals, weighted_sums = lax.map(forward_rows, pix_split)
    peaks = peaks.reshape(capacity, H)
    totals = totals.reshape(capacity, H)
    weighted_sums = weighted_sums.reshape(capacity, H, DH)
    upstream = out_grad.astype(jnp.float32).reshape(capacity, H, DH) * filled[:, None, None]
    heads_local = H // var_devices
    first_head = lax.axis_index("vars") * heads_local

    def combine(first, second):
        peak_both = jnp.maximum(first[0], second[0])
        left_factor = jnp.exp(first[0] - peak_both)
        right_factor = jnp.exp(second[0] - peak_both)
        return (
            peak_both,
            first[1] * left_factor + second[1] * right_factor,
            first[2] * left_factor[:, :, None] + second[2] * right_factor[:, :, None],
        )

    peak_all, summed, weighted_all = combined_all((peaks, totals, weighted_sums), "vars", combine)
    mixture = weighted_all / summed[:, :, None]
    inner_out = jnp.sum(upstream * mixture, axis=2)
    own_heads = lax.dynamic_slice_in_dim(mixture, first_head, heads_local, 1)
    tokens = (
        (own_heads * filled[:, None, None]).reshape(capacity, heads_local * DH).astype(jnp.bfloat16)
    )

    def backward_rows(running, pieces):
        weight_acc, bias_acc, query_acc = running
        stored_rows, pix_rows, peak_rows, total_rows, inner_rows, grad_rows = pieces
        embedded = embed_rows(stored_rows)
        head_view, scores = head_scores(embedded)
        attention = jnp.exp(scores - peak_rows[:, :, None]) / total_rows[:, :, None]
        grad_attn = jnp.einsum("she,svhe->shv", grad_rows, head_view, precision=high)
        grad_score = attention * (grad_attn - inner_rows[:, :, None])
        grad_embed = (
            jnp.einsum("shv,she->svhe", attention, grad_rows, precision=high)
            + jnp.einsum("shv,he->svhe", grad_score, agg_query, precision=high) * score_scale
        )
        grad_embed = grad_embed.reshape(row_block, var_local, D)
        grad_low = grad_embed.astype(jnp.bfloat16)
        weight_acc = weight_acc + jnp.einsum(
            "svp,svd->vpd", pix_rows, grad_low, preferred_element_type=jnp.float32
        )
        bias_acc = bias_acc + jnp.sum(grad_embed, axis=0)
        query_acc = (
            query_acc
            + jnp.einsum("shv,svhe->he", grad_score, head_view, precision=high) * score_scale
        )
        grad_pixels = jnp.einsum(
            "svd,vpd->svp", grad_low, embed_weight, preferred_element_type=jnp.float32
        ).astype(jnp.bfloat16)
        return ((weight_acc, bias_acc, query_acc), grad_pixels)

    start_sums = (
        jnp.zeros((var_local, P_SIZE, D), jnp.float32),
        jnp.zeros((var_local, D), jnp.float32),
        jnp.zeros((H, DH), jnp.float32),
    )
    scan_inputs = (
        pix_split,
        pix_split,
        peak_all.reshape(block_count, row_block, H),
        summed.reshape(block_count, row_block, H),
        inner_out.reshape(block_count, row_block, H),
        upstream.reshape(block_count, row_block, H, DH),
    )
    sums_final, grad_pixels = lax.scan(backward_rows, start_sums, scan_inputs)
    weight_acc, bias_acc, query_acc = sums_final
    returned = lax.all_to_all(
        grad_pixels.reshape(row_devices, slot_depth, var_local * P_SIZE),
        "rows",
        split_axis=0,
        concat_axis=0,
        tiled=True,
    )
    grad_patches = returned.reshape(capacity, var_local * P_SIZE)[target]
    grad_blocks = (
        grad_patches.reshape(blocks, PB, var_local, P_SIZE)
        .transpose(0, 2, 1, 3)
        .reshape(blocks, var_local, block_pixels)
    )

    def backward_block(pieces):
        grad_block, index_rows, weight_rows = pieces
        matrix = interp_matrix(index_rows, weight_rows)
        return jnp.dot(grad_block, matrix, preferred_element_type=jnp.float32)

    field_grad = (
        lax.map(backward_block, (grad_blocks, index_blocks, weight_blocks))
        .transpose(1, 0, 2)
        .reshape(var_local, point_count)
    )
    weight_grad, bias_grad = lax.psum((weight_acc, bias_acc), "rows")
    query_grad = lax.psum(query_acc, ("rows", "vars"))
    return (tokens, field_grad, weight_grad, bias_grad, query_grad)


def solution(mesh):
    return jax.shard_map(
        local,
        mesh=mesh,
        in_specs=(
            P("vars", "rows"),
            P("rows", None),
            P("rows", None),
            P("rows", None),
            P("vars", None, None),
            P("vars", None),
            P(),
            P("rows", None),
        ),
        out_specs=(
            P("rows", "vars"),
            P("vars", "rows"),
            P("vars", None, None),
            P("vars", None),
            P(),
        ),
        check_vma=False,
    )
```

profile of v0, /device:TPU:0, one launch (start us, length us, event | category | flops | bytes accessed | tf_op | source)
XLA Modules:
  0.0 239.4 jit_solution(9300572705126652335)
XLA Ops:
  7.2 0.8 fusion.41
  8.1 0.8 select_reduce_fusion
  9.0 0.7 fusion.47
  9.6 14.3 %while.4 = (s32[]{:T(128)}, bf16[4,8,512]{2,1,0:T(8,128)(2,1)S(1)}, bf16[4,8,1024]{2,1,0:T(8,128)(2,1)}, s32[4,512,4]{1,2,0:T(4,128)}, f32[4,512,4]{1,2,0:T(4,128)}, /*index=5*/s32[]{:T(128)}) while((s32[]{:T(128)}, bf16[4,8,512]{2,1,0:T(8,128)(2,1)S(1)}, bf16[4,8,1024]{2,1,0:T(8,128)(2,1)}, s32[4,512,4]{1,2,0:T(4,128)}, ...), condition=%wide.region_3.4_spmd, body=%wide.region_2.3_spmd.sunk | while | flops 14684162 | bytes 107597 | solution.py:62
  9.6 0.7 dynamic-slice_bitcast_fusion.8
  10.4 0.7 dynamic-slice_bitcast_fusion.9
  11.1 2.1 fusion.77
  13.2 0.7 dynamic-slice_bitcast_fusion.8
  13.9 0.7 dynamic-slice_bitcast_fusion.9
  14.7 2.1 fusion.77
  16.8 0.7 dynamic-slice_bitcast_fusion.8
  17.5 0.7 dynamic-slice_bitcast_fusion.9
  18.2 2.1 fusion.77
  20.4 0.7 dynamic-slice_bitcast_fusion.8
  21.1 0.7 dynamic-slice_bitcast_fusion.9
  21.8 2.1 fusion.77
  23.9 0.2 reshape.147
  24.6 1.5 scatter_custom_fusion
  26.1 8.3 %all-to-all-start = ((bf16[16,16,128]{2,1,0:T(8,128)(2,1)}), bf16[16,16,128]{2,1,0:T(8,128)(2,1)S(1)}, u32[]{:S(2)}, u32[]{:S(2)}) async-start(bf16[16,16,128]{2,1,0:T(8,128)(2,1)} %bitcast.34), calls=%async_computation | async-start | bytes 131072 | tf_op jit(solution)/shard_map/all_to_all | solution.py:79
  34.5 7.5 %all-to-all-done = bf16[16,16,128]{2,1,0:T(8,128)(2,1)S(1)} async-done(((bf16[16,16,128]{2,1,0:T(8,128)(2,1)}), bf16[16,16,128]{2,1,0:T(8,128)(2,1)S(1)}, u32[]{:S(2)}, u32[]{:S(2)}) %all-to-all-start) | async-done | bytes 65568 | tf_op jit(solution)/shard_map/all_to_all | solution.py:79
  41.9 0.4 squeeze.62
  42.3 0.3 copy.29
  42.6 3.3 %fusion.29 = bf16[256,8,1024]{2,0,1:T(8,128)(2,1)} fusion(f32[8,1024]{1,0:T(8,128)S(1)} %convert_element_type.60, bf16[256,8,16]{0,2,1:T(8,128)(2,1)S(1)} %copy.29, bf16[8,16,1024]{2,1,0:T(8,128)(2,1)S(1)} %copy-done), kind=kOutput, calls=%fused_computation.52 | convolution fusion | flops 71303168 | bytes 4554752 | tf_op jit(solution)/shard_map/while/body/eval_jaxpr/svp,vpd->svd/dot_general | solution.py:101
  45.9 6.4 %copy.30 = bf16[256,8,1024]{0,2,1:T(8,128)(2,1)} copy(bf16[256,8,1024]{2,0,1:T(8,128)(2,1)} %fusion.29) | data formatting | bytes 8388608 | tf_op jit(solution)/shard_map/while/body/eval_jaxpr/convert_element_type | solution.py:104
  52.3 4.1 %fusion.32 = f32[16,1,256,8]{2,1,3,0:T(1,128)S(1)} fusion(f32[16,64,1,1]{1,2,3,0:T(1,128)S(1)} %bitcast.209, bf16[256,8,16,64]{0,3,2,1:T(8,128)(2,1)} %bitcast.182), kind=kOutput, calls=%fused_computation.55 | convolution fusion | flops 25165824 | bytes 4329472 | tf_op jit(solution)/shard_map/while/body/eval_jaxpr/svhe,he->shv/dot_general | solution.py:110
  56.5 2.2 multiply_reduce_fusion.1
  58.8 1.3 scatter_custom_fusion.1
  60.1 0.7 all_to_all.16
  60.8 3.5 %all-to-all-start.1 = ((bf16[16,1,16]{2,1,0:T(2,128)(2,1)}), bf16[16,1,16]{2,1,0:T(2,128)(2,1)S(1)}, u32[]{:S(2)}, u32[]{:S(2)}) async-start(bf16[16,1,16]{2,1,0:T(2,128)(2,1)} %all_to_all.16), calls=%async_computation.1 | async-start | bytes 16384 | tf_op jit(solution)/shard_map/all_to_all | solution.py:86
  64.4 0.2 copy.32
  64.6 6.9 %all-to-all-done.1 = bf16[16,1,16]{2,1,0:T(2,128)(2,1)S(1)} async-done(((bf16[16,1,16]{2,1,0:T(2,128)(2,1)}), bf16[16,1,16]{2,1,0:T(2,128)(2,1)S(1)}, u32[]{:S(2)}, u32[]{:S(2)}) %all-to-all-start.1) | async-done | bytes 544 | tf_op jit(solution)/shard_map/all_to_all | solution.py:86
  71.6 1.8 all-gather.1
  73.4 2.0 all-gather.2
  75.5 2.1 multiply_reduce_fusion.2
  77.6 0.7 copy-done.2
  78.3 1.6 multiply_reduce_fusion
  80.0 2.1 fusion.27
  82.0 2.0 copy-done.4
  84.0 2.0 fusion.58
  86.0 3.0 %fusion.34 = bf16[256,8,16]{0,2,1:T(8,128)(2,1)S(1)} fusion(bf16[8,16,1024]{2,1,0:T(8,128)(2,1)S(1)} %copy-done, bf16[256,8,1024]{0,2,1:T(8,128)(2,1)} %bitcast.186), kind=kOutput, calls=%fused_computation.58 | convolution fusion | flops 67141632 | bytes 4521984 | tf_op jit(solution)/shard_map/while/body/eval_jaxpr/svd,vpd->svp/dot_general | solution.py:169
  89.0 0.5 copy-done.3
  89.4 3.4 %fusion.30 = f32[16,1,64,1]{2,1,3,0:T(1,128)S(1)} fusion(bf16[256,8,16,64]{0,3,2,1:T(8,128)(2,1)S(1)} %bitcast.184, f32[256,16,8,1]{0,1,2,3:T(8,128)S(1)} %get-tuple-element.175), kind=kOutput, calls=%fused_computation.53 | convolution fusion | flops 25165824 | bytes 4329472 | tf_op jit(solution)/shard_map/while/body/eval_jaxpr/shv,svhe->he/dot_general | solution.py:167
  92.9 0.4 reshape.208
  93.2 1.0 copy.60
  94.3 3.5 %all-to-all-start.2 = ((bf16[16,16,128]{2,1,0:T(8,128)(2,1)}), bf16[16,16,128]{2,1,0:T(8,128)(2,1)S(1)}, u32[]{:S(2)}, u32[]{:S(2)}) async-start(bf16[16,16,128]{2,1,0:T(8,128)(2,1)} %copy.60), calls=%async_computation.2 | async-start | bytes 131072 | tf_op jit(solution)/shard_map/all_to_all | solution.py:189
  97.9 0.8 copy.39
  98.8 40.6 %psum.23 = f32[16,64]{1,0:T(8,128)} all-reduce(f32[16,64]{1,0:T(8,128)S(1)} %broadcast_multiply_fusion), channel_id=1, replica_groups=mesh['rows'=16,'vars'=2] {'rows','vars'}, use_global_device_ids=true, to_apply=%region_14.15 | all-reduce | flops 1024 | bytes 8192 | tf_op jit(solution)/shard_map/psum | solution.py:214
  139.4 76.8 %psum.22 = f32[8,1024]{1,0:T(8,128)} all-reduce(f32[8,1024]{1,0:T(8,128)S(1)} %reduce_sum.47), channel_id=1, replica_groups=mesh['rows'=16,'vars'=2] {'rows'}, use_global_device_ids=true, to_apply=%region_13.14 | all-reduce | flops 8192 | bytes 65536 | tf_op jit(solution)/shard_map/psum | solution.py:213
  216.1 0.7 gather_fusion
  217.3 0.3 reshape.156
  217.6 13.0 %while.5 = (s32[]{:T(128)}, f32[4,8,1024]{2,1,0:T(8,128)}, bf16[4,8,512]{2,1,0:T(8,128)(2,1)S(1)}, s32[4,512,4]{1,2,0:T(4,128)}, f32[4,512,4]{1,2,0:T(4,128)}, /*index=5*/s32[]{:T(128)}) while((s32[]{:T(128)}, f32[4,8,1024]{2,1,0:T(8,128)}, bf16[4,8,512]{2,1,0:T(8,128)(2,1)S(1)}, s32[4,512,4]{1,2,0:T(4,128)}, f32[4,512,4]{1,2,0:T(4,128)}, ...), condition=%wide.region_10.11_spmd, body=%wide.region_9.10_spmd.sunk | while | flops 14680066 | bytes 123981 | solution.py:209
  217.6 0.7 dynamic-slice_bitcast_fusion.10
  218.3 0.7 dynamic-slice_bitcast_fusion.11
  219.0 1.8 fusion.81
  220.9 0.7 dynamic-slice_bitcast_fusion.10
  221.6 0.7 dynamic-slice_bitcast_fusion.11
  222.3 1.8 fusion.81
  224.1 0.7 dynamic-slice_bitcast_fusion.10
  224.8 0.7 dynamic-slice_bitcast_fusion.11
  225.5 1.8 fusion.81
  227.4 0.7 dynamic-slice_bitcast_fusion.10
  228.1 0.7 dynamic-slice_bitcast_fusion.11
  228.8 1.8 fusion.81
  230.6 1.9 copy.95
  (58 shorter events, 1.8 us)
Async XLA Ops:
  7.2 35.4 %copy-start = (bf16[8,16,1024]{2,1,0:T(8,128)(2,1)S(1)}, bf16[8,16,1024]{2,1,0:T(8,128)(2,1)}, u32[]{:S(2)}) copy-start(bf16[8,16,1024]{2,1,0:T(8,128)(2,1)} %param.16) | copy-start | bytes 786436
  9.6 24.8 %copy-start.6 = (bf16[8,1024]{1,0:T(8,128)(2,1)S(1)}, bf16[8,1024]{1,0:T(8,128)(2,1)}, u32[]{:S(2)}) copy-start(bf16[8,1024]{1,0:T(8,128)(2,1)} %param.17) | copy-start | bytes 49156
  26.1 15.9 %all-to-all-start = ((bf16[16,16,128]{2,1,0:T(8,128)(2,1)}), bf16[16,16,128]{2,1,0:T(8,128)(2,1)S(1)}, u32[]{:S(2)}, u32[]{:S(2)}) async-start(bf16[16,16,128]{2,1,0:T(8,128)(2,1)} %bitcast.34), calls=%async_computation | async-start | bytes 131072 | tf_op jit(solution)/shard_map/all_to_all | solution.py:79
  34.4 41.1 %all-gather.5.cloned.1.call-start = ((), (), s32[]{:S(2)}) async-start(), calls=%async_computation.4 | async-start | bytes 3145728 | tf_op jit(solution)/shard_map/all_gather | solution.py:18
  45.9 6.5 %copy-start.7 = (f32[16,64]{1,0:T(8,128)S(1)}, f32[16,64]{1,0:T(8,128)}, u32[]{:S(2)}) copy-start(f32[16,64]{1,0:T(8,128)} %param.18) | copy-start | bytes 12292
  52.3 4.2 %copy-start.1 = (bf16[256,8,1024]{0,2,1:T(8,128)(2,1)S(1)}, bf16[256,8,1024]{0,2,1:T(8,128)(2,1)}, u32[]{:S(2)}) copy-start(bf16[256,8,1024]{0,2,1:T(8,128)(2,1)} %copy.30) | copy-start | bytes 12582916
  56.5 7.9 %copy-start.5 = (bf16[256,1024]{1,0:T(8,128)(2,1)S(1)}, bf16[256,1024]{1,0:T(8,128)(2,1)}, u32[]{:S(2)}) copy-start(bf16[256,1024]{1,0:T(8,128)(2,1)} %param.19) | copy-start | bytes 1572868
  60.8 10.7 %all-to-all-start.1 = ((bf16[16,1,16]{2,1,0:T(2,128)(2,1)}), bf16[16,1,16]{2,1,0:T(2,128)(2,1)S(1)}, u32[]{:S(2)}, u32[]{:S(2)}) async-start(bf16[16,1,16]{2,1,0:T(2,128)(2,1)} %all_to_all.16), calls=%async_computation.1 | async-start | bytes 16384 | tf_op jit(solution)/shard_map/all_to_all | solution.py:86
  64.3 166.3 %all-reduce.2.cloned.1.call-start = ((), (), s32[]{:S(2)}) async-start(), calls=%async_computation.3 | async-start | bytes 1048576 | tf_op jit(solution)/shard_map/psum | solution.py:213
  75.4 2.8 %copy-start.2 = (bf16[256,8,1024]{0,2,1:T(8,128)(2,1)S(1)}, bf16[256,8,1024]{0,2,1:T(8,128)(2,1)}, u32[]{:S(2)}) copy-start(bf16[256,8,1024]{0,2,1:T(8,128)(2,1)} %copy.30) | copy-start | bytes 12582916
  82.0 2.0 copy-start.4
  86.0 3.4 %copy-start.3 = (bf16[256,8,1024]{0,2,1:T(8,128)(2,1)S(1)}, bf16[256,8,1024]{0,2,1:T(8,128)(2,1)}, u32[]{:S(2)}) copy-start(bf16[256,8,1024]{0,2,1:T(8,128)(2,1)} %copy.30) | copy-start | bytes 12582916
  94.3 121.9 %all-to-all-start.2 = ((bf16[16,16,128]{2,1,0:T(8,128)(2,1)}), bf16[16,16,128]{2,1,0:T(8,128)(2,1)S(1)}, u32[]{:S(2)}, u32[]{:S(2)}) async-start(bf16[16,16,128]{2,1,0:T(8,128)(2,1)} %copy.60), calls=%async_computation.2 | async-start | bytes 131072 | tf_op jit(solution)/shard_map/all_to_all | solution.py:189
Sparse Core Ops, SparseCore 0:
  58.9 7.3 all-gather.4
  93.0 105.0 all-reduce.1
where the time goes:
time: 241 us; the launch traced here: 239 us
  blocking collectives  121 us (50%)
  local copies, waits for them, and re-layouts  31.8 us (13%)
  matrix products  31.6 us (13%)
  starting transfers between devices  15.4 us (6%)
  waiting for transfers between devices  14.4 us (6%)
  between operations  14.3 us (6%)
  other arithmetic  10.7 us (4%)
    psum x1, blocking collectives, local(): weight_grad, bias_grad = lax.psum((weight_acc, bias_acc), 'rows')  76.8 us
    psum x1, blocking collectives, local(): query_grad = lax.psum(query_acc, ('rows', 'vars'))  40.6 us
    squeeze x16, local copies, waits for them, and re-layouts, local(): pixels = lax.map(forward_block, (field_blocks, index_blocks, weight_blocks))  11.3 us
    dot_general x4, matrix products, forward_block(): jnp.dot(field_block, matrix.T, preferred_element_type=jnp.float32)  8.54 us
    all_to_all x1, starting transfers between devices, local(): lax.all_to_all(outbox.reshape(row_devices, slot_depth, var_local * P_SIZE...  8.31 us
    all_to_all x1, waiting for transfers between devices, local(): lax.all_to_all(outbox.reshape(row_devices, slot_depth, var_local * P_SIZE...  7.46 us
    dot_general x4, matrix products, backward_block(): return jnp.dot(grad_block, matrix, preferred_element_type=jnp.float32)  7.33 us
    all_to_all x1, waiting for transfers between devices, local(): lax.all_to_all(markers.reshape(row_devices, slot_depth), 'rows', split_ax...  6.87 us
  transfers between devices with their start and end apart: 5, of which 2 were waited for; matrix products, arithmetic and copies ran while one was open for 8% of the time, Pallas kernels for 0%

commit v1 on v0

v1 whole, which is shorter than its diff:
```python
import functools
import math

import jax
import jax.numpy as jnp
from jax import lax
from jax.experimental import pallas as pl
from jax.experimental.pallas import tpu as pltpu
from jax.sharding import PartitionSpec as P

D = 1024
H = 16
DH = 64
P_SIZE = 16
K = 4
PTS_BLK = 1024
PB = 32
LANE = 128
SUB = 8
J_STEP = 64
MESH = pl.DeviceIdType.MESH
F32 = jnp.float32
BF16 = jnp.bfloat16


def nn(a, b):
    return lax.dot_general(a, b, (((1,), (0,)), ((), ())), preferred_element_type=F32)


def nt(a, b):
    return lax.dot_general(a, b, (((1,), (1,)), ((), ())), preferred_element_type=F32)


def iota(shape, axis):
    return lax.broadcasted_iota(jnp.int32, shape, axis)


def split_two(x):
    high = x.astype(BF16)
    return high, (x - high.astype(F32)).astype(BF16)


def expand(x, spread):
    high, low = split_two(x)
    return nn(high, spread) + nn(low, spread)


def aligned(start, size):
    return pl.ds(pl.multiple_of(start * size, size), size)


def kernel(
    n_rows, n_vars, var_local, blocks, depth,
    fields, stencil, stencil_weight, owner_col, owner_row, weight, bias, query, out_grad,
    tok_out, field_out, weight_out, bias_out, query_out,
    arrived, matrix, spread_fields, up, pix_t, emb, scores, attn_grad,
    mix_send, mix_recv, stat, tok_send, bias_sum, query_part, part_send, part_recv,
    small_send, small_recv, done,
    og_s, og_r, sw_s, sw_r, mx_s, mx_r, st_s, st_r, tk_s, tk_r, qp_s, qp_r,
    pt_s, pt_r, sm_s, sm_r, dn_s, dn_r,
):
    me = lax.axis_index("rows")
    mine = lax.axis_index("vars")
    patches = blocks * PB
    vp = var_local * P_SIZE
    width = D // n_vars
    slots = n_rows * depth
    block_pixels = PB * P_SIZE
    scale = 1.0 / math.sqrt(DH)
    tiles = vp // SUB * (D // LANE) // n_rows

    def row_dev(peer):
        return (peer, mine)

    def var_dev(peer):
        return (me, peer)

    def copy(src, dst, send, recv, device):
        return pltpu.make_async_remote_copy(
            src_ref=src, dst_ref=dst, send_sem=send, recv_sem=recv,
            device_id=device, device_id_type=MESH,
        )

    def each_row(body):
        def step(i, carry):
            body(lax.rem(me + i, n_rows))
            return carry

        lax.fori_loop(1, n_rows, step, 0)

    def each_var(body):
        for i in range(1, n_vars):
            body(lax.rem(mine + i, n_vars))

    barrier = pltpu.get_barrier_semaphore()
    each_row(
        lambda p: pl.semaphore_signal(barrier, inc=1, device_id=row_dev(p), device_id_type=MESH)
    )
    each_var(
        lambda p: pl.semaphore_signal(barrier, inc=1, device_id=var_dev(p), device_id_type=MESH)
    )
    pl.semaphore_wait(barrier, n_rows + n_vars - 2)

    own_lanes = pl.ds(pl.multiple_of(mine * width, LANE), width)

    def og_copy(src_row, dst_row, send, recv, p):
        return copy(
            out_grad.at[aligned(src_row, depth), own_lanes],
            arrived.at[mine, aligned(dst_row, depth), :],
            og_s.at[send], og_r.at[recv], row_dev(p),
        )

    each_row(lambda p: og_copy(p, me, p, me, p).start())
    arrived[mine, aligned(me, depth), :] = out_grad[aligned(me, depth), own_lanes]

    def own_pixel(shape, row_axis):
        return iota(shape, 0) % P_SIZE == iota(shape, 1) % P_SIZE

    def placing(b):
        shape = (patches, block_pixels)
        return (iota(shape, 0) == b * PB + iota(shape, 1) // P_SIZE).astype(F32).astype(BF16)

    def interp(b, pix):
        columns = aligned(b, block_pixels)
        index_rows = stencil[:, columns]
        weight_rows = stencil_weight[:, columns]

        def chunk(j, carry):
            points = j * J_STEP + iota((J_STEP, block_pixels), 0)
            total = jnp.zeros((J_STEP, block_pixels), F32)
            for entry in range(K):
                total = total + jnp.where(
                    index_rows[entry : entry + 1] == points,
                    weight_rows[entry : entry + 1],
                    0.0,
                )
            matrix[b, aligned(j, J_STEP), :] = total.astype(BF16)
            return carry

        lax.fori_loop(0, PTS_BLK // J_STEP, chunk, 0)
        block_fields = fields[:, aligned(b, PTS_BLK)].astype(F32)
        for v in range(var_local):
            spread_fields[v * P_SIZE : (v + 1) * P_SIZE, :] = jnp.broadcast_to(
                block_fields[v : v + 1], (P_SIZE, PTS_BLK)
            ).astype(BF16)
        values = nn(spread_fields[...], matrix[b]).astype(BF16).astype(F32)
        kept = jnp.where(own_pixel((vp, block_pixels), 0), values, 0.0).astype(BF16)
        return pix + nt(placing(b), kept)

    pix = lax.fori_loop(0, blocks, interp, jnp.zeros((patches, vp), F32))
    pix_t[...] = pix.T.astype(BF16)

    square = (patches, patches)
    same = owner_col[...] == owner_row[...]
    rank_col = jnp.sum(
        jnp.where(same & (iota(square, 1) < iota(square, 0)), 1.0, 0.0), axis=1, keepdims=True
    ).astype(jnp.int32)
    rank_row = jnp.sum(
        jnp.where(same & (iota(square, 0) < iota(square, 1)), 1.0, 0.0), axis=0, keepdims=True
    ).astype(jnp.int32)
    slot_col = owner_col[...] * depth + rank_col
    slot_row = owner_row[...] * depth + rank_row
    take = (slot_col == iota((patches, slots), 1)).astype(F32).astype(BF16)
    put = (slot_row == iota((slots, patches), 0)).astype(F32).astype(BF16)

    each_row(lambda p: og_copy(p, p, p, p, p).wait_recv())

    def swap_copy(part, sem_s, sem_r, p):
        return copy(arrived.at[part], arrived.at[part], sw_s.at[sem_s], sw_r.at[sem_r], var_dev(p))

    each_var(lambda p: swap_copy(mine, p, mine, p).start())

    heads = iota((H, D), 0) == iota((H, D), 1) // DH
    spread = heads.astype(F32).astype(BF16)
    own_heads = iota((H, width), 0) == (mine * width + iota((H, width), 1)) // DH
    own_spread = own_heads.astype(F32).astype(BF16)
    query_wide = jnp.where(heads, query[...], 0.0)
    query_a = query_wide.astype(BF16)
    rest = query_wide - query_a.astype(F32)
    query_b = rest.astype(BF16)
    query_c = (rest - query_b.astype(F32)).astype(BF16)

    def embed(v, carry):
        mask = iota((patches, vp), 1) // P_SIZE == v
        own = jnp.where(mask, pix, 0.0).astype(BF16)
        low = (nn(own, weight[...]) + bias[pl.ds(v, 1), :]).astype(BF16)
        emb[v] = low
        scores[v] = (nt(low, query_a) + nt(low, query_b) + nt(low, query_c)) * scale
        return carry

    lax.fori_loop(0, var_local, embed, 0)
    each_var(lambda p: swap_copy(p, p, p, p).wait_recv())
    for part in range(n_vars):
        up[:, part * width : (part + 1) * width] = nn(take, arrived[part])

    peak = jnp.max(scores[...], axis=0)

    def gather(v, carry):
        total, inner, mixed = carry
        values = emb[v].astype(F32)
        high, low = split_two(up[...] * values)
        grad = nt(high, spread) + nt(low, spread)
        attn_grad[v] = grad
        power = jnp.exp(scores[v] - peak)
        scores[v] = power
        return total + power, inner + power * grad, mixed + expand(power, spread) * values

    nothing = jnp.zeros((patches, H), F32)
    total, inner, mixed = lax.fori_loop(
        0, var_local, gather, (nothing, nothing, jnp.zeros((patches, D), F32))
    )
    stat[mine, 0] = peak
    stat[mine, 1] = total
    stat[mine, 2] = inner
    for part in range(n_vars):
        mix_send[part] = mixed[:, part * width : (part + 1) * width]

    def stat_copy(part, sem_s, sem_r, p):
        return copy(stat.at[part], stat.at[part], st_s.at[sem_s], st_r.at[sem_r], var_dev(p))

    def mix_copy(part, slot, sem_s, sem_r, p):
        return copy(
            mix_send.at[part], mix_recv.at[slot], mx_s.at[sem_s], mx_r.at[sem_r], var_dev(p)
        )

    each_var(lambda p: stat_copy(mine, p, mine, p).start())
    each_var(lambda p: mix_copy(p, mine, p, mine, p).start())
    mix_recv[mine] = mix_send[mine]
    each_var(lambda p: stat_copy(p, p, p, p).wait_recv())
    peak_all = stat[0, 0]
    for part in range(1, n_vars):
        peak_all = jnp.maximum(peak_all, stat[part, 0])
    factors = [jnp.exp(stat[part, 0] - peak_all) for part in range(n_vars)]
    total_all = sum(stat[part, 1] * factors[part] for part in range(n_vars))
    inner_all = sum(stat[part, 2] * factors[part] for part in range(n_vars)) / total_all
    own_factor = jnp.exp(peak - peak_all) / total_all

    each_var(lambda p: mix_copy(p, p, p, p, p).wait_recv())
    mixture = sum(
        expand(factors[part] / total_all, own_spread) * mix_recv[part] for part in range(n_vars)
    )
    tok_send[...] = nn(put, mixture.astype(BF16)).astype(BF16)

    def tok_copy(src_row, dst_row, send, recv, p):
        return copy(
            tok_send.at[aligned(src_row, depth), :], tok_out.at[aligned(dst_row, depth), :],
            tk_s.at[send], tk_r.at[recv], row_dev(p),
        )

    each_row(lambda p: tok_copy(p, me, p, me, p).start())
    tok_out[aligned(me, depth), :] = tok_send[aligned(me, depth), :]

    query_scaled = query[...] * scale

    def part_copy(slot_s, slot_r, send, recv, p):
        return copy(
            part_send.at[slot_s], part_recv.at[slot_r], pt_s.at[send], pt_r.at[recv], row_dev(p)
        )

    per_group = D // LANE // tiles
    per_var = P_SIZE // SUB * per_group

    def backward(i, carry):
        pix_grad, query_sum = carry
        v = lax.rem(i + me // per_var, var_local)
        values = emb[v].astype(F32)
        attention = scores[v] * own_factor
        score_grad = attention * (attn_grad[v] - inner_all)
        score_wide = expand(score_grad, spread)
        grad = expand(attention, spread) * up[...] + score_wide * query_scaled
        low = grad.astype(BF16)
        bias_sum[v] = jnp.sum(grad, axis=0, keepdims=True)
        query_sum = query_sum + jnp.sum(score_wide * values, axis=0, keepdims=True)
        found = nn(pix_t[aligned(v, P_SIZE), :], low)
        for group in range(P_SIZE // SUB):
            for lane in range(D // LANE):
                slot = v * per_var + group * per_group + lane // tiles
                part_send[slot, lane % tiles] = found[
                    group * SUB : (group + 1) * SUB, lane * LANE : (lane + 1) * LANE
                ]
        for step in range(per_var):
            slot = v * per_var + step

            @pl.when(slot != me)
            def _():
                part_copy(slot, me, slot, me, slot).start()

        mask = iota((patches, vp), 1) // P_SIZE == v
        pix_grad = pix_grad + jnp.where(mask, nt(low, weight[...]), 0.0)
        return pix_grad, query_sum

    pix_grad, query_sum = lax.fori_loop(
        0, var_local, backward, (jnp.zeros((patches, vp), F32), jnp.zeros((1, D), F32))
    )
    part_recv[me] = part_send[me]

    query_part[mine] = jnp.broadcast_to(query_sum * scale, (SUB, D))

    def query_copy(part, sem_s, sem_r, p):
        return copy(
            query_part.at[part], query_part.at[part], qp_s.at[sem_s], qp_r.at[sem_r], var_dev(p)
        )

    each_var(lambda p: query_copy(mine, p, mine, p).start())

    grad_t = pix_grad.T.astype(BF16)
    pick = (iota((var_local, vp), 0) == iota((var_local, vp), 1) // P_SIZE).astype(F32).astype(BF16)

    small_send[...] = jnp.zeros_like(small_send)
    bias_tiles = var_local // SUB * (D // LANE)
    for group in range(var_local // SUB):
        rows = jnp.concatenate([bias_sum[group * SUB + k] for k in range(SUB)], axis=0)
        for lane in range(D // LANE):
            small_send[group * (D // LANE) + lane] = rows[:, lane * LANE : (lane + 1) * LANE]
    each_var(lambda p: query_copy(p, p, p, p).wait_recv())
    query_all = query_part[0]
    for part in range(1, n_vars):
        query_all = query_all + query_part[part]
    for lane in range(D // LANE):
        small_send[bias_tiles + lane] = query_all[:, lane * LANE : (lane + 1) * LANE]

    def small_copy(slot_s, slot_r, send, recv, p):
        return copy(
            small_send.at[slot_s], small_recv.at[slot_r], sm_s.at[send], sm_r.at[recv], row_dev(p)
        )

    each_row(lambda p: small_copy(p, me, p, me, p).start())
    small_recv[me] = small_send[me]

    def field_block(b, carry):
        values = nn(grad_t, placing(b))
        kept = jnp.where(own_pixel((vp, block_pixels), 0), values, 0.0).astype(BF16)
        by_pixel = nn(pick, kept).astype(BF16)
        field_out[:, aligned(b, PTS_BLK)] = nt(by_pixel, matrix[b])
        return carry

    lax.fori_loop(0, blocks, field_block, 0)

    each_row(lambda p: part_copy(p, p, p, p, p).wait_recv())
    each_row(lambda p: small_copy(p, p, p, p, p).wait_recv())
    done[me, 0:tiles] = jnp.sum(part_recv[...], axis=0)
    done[me, tiles] = jnp.sum(small_recv[...], axis=0)

    def done_copy(slot, send, recv, p):
        return copy(done.at[slot], done.at[slot], dn_s.at[send], dn_r.at[recv], row_dev(p))

    each_row(lambda p: done_copy(me, p, me, p).start())
    each_row(lambda p: done_copy(p, p, p, p).wait_recv())
    for slot in range(n_rows):
        for tile in range(tiles):
            number = slot * tiles + tile
            group, lane = number // (D // LANE), number % (D // LANE)
            weight_out[group * SUB : (group + 1) * SUB, lane * LANE : (lane + 1) * LANE] = done[
                slot, tile
            ]
    for number in range(bias_tiles):
        group, lane = number // (D // LANE), number % (D // LANE)
        bias_out[group * SUB : (group + 1) * SUB, lane * LANE : (lane + 1) * LANE] = done[
            number, tiles
        ]
    for lane in range(D // LANE):
        query_out[:, lane * LANE : (lane + 1) * LANE] = done[bias_tiles + lane, tiles]

    each_row(lambda p: tok_copy(p, p, p, p, p).wait_recv())
    each_row(lambda p: og_copy(p, me, p, me, p).wait_send())
    each_row(lambda p: tok_copy(p, me, p, me, p).wait_send())
    each_row(lambda p: part_copy(p, me, p, me, p).wait_send())
    each_row(lambda p: small_copy(p, me, p, me, p).wait_send())
    each_row(lambda p: done_copy(me, p, me, p).wait_send())
    each_var(lambda p: swap_copy(mine, p, mine, p).wait_send())
    each_var(lambda p: stat_copy(mine, p, mine, p).wait_send())
    each_var(lambda p: mix_copy(p, mine, p, mine, p).wait_send())
    each_var(lambda p: query_copy(mine, p, mine, p).wait_send())


def local(
    fields, stencil, stencil_weight, owner_map, embed_weight, embed_bias, agg_query, out_grad
):
    n_rows = lax.axis_size("rows")
    n_vars = lax.axis_size("vars")
    var_local, points = fields.shape
    blocks = points // PTS_BLK
    patches = owner_map.shape[0]
    capacity = out_grad.shape[0]
    slot_depth = capacity // n_rows
    depth = -(-slot_depth // 16) * 16
    vp = var_local * P_SIZE
    width = D // n_vars
    slots = n_rows * depth
    tiles = vp // SUB * (D // LANE) // n_rows
    if depth != slot_depth:
        out_grad = jnp.pad(
            out_grad.reshape(n_rows, slot_depth, D), ((0, 0), (0, depth - slot_depth), (0, 0))
        ).reshape(slots, D)
    vmem = pl.BlockSpec(memory_space=pltpu.VMEM)
    dma = pltpu.SemaphoreType.DMA
    row_sem, var_sem = dma((n_rows,)), dma((n_vars,))
    tokens, field_grad, weight_grad, bias_grad, query_grad = pl.pallas_call(
        functools.partial(kernel, n_rows, n_vars, var_local, blocks, depth),
        out_shape=(
            jax.ShapeDtypeStruct((slots, width), BF16),
            jax.ShapeDtypeStruct((var_local, points), F32),
            jax.ShapeDtypeStruct((vp, D), F32),
            jax.ShapeDtypeStruct((var_local, D), F32),
            jax.ShapeDtypeStruct((SUB, D), F32),
        ),
        in_specs=[vmem] * 9,
        out_specs=(vmem,) * 5,
        scratch_shapes=[
            pltpu.VMEM((n_vars, slots, width), BF16),
            pltpu.VMEM((blocks, PTS_BLK, PB * P_SIZE), BF16),
            pltpu.VMEM((vp, PTS_BLK), BF16),
            pltpu.VMEM((patches, D), F32),
            pltpu.VMEM((vp, patches), BF16),
            pltpu.VMEM((var_local, patches, D), BF16),
            pltpu.VMEM((var_local, patches, H), F32),
            pltpu.VMEM((var_local, patches, H), F32),
            pltpu.VMEM((n_vars, patches, width), F32),
            pltpu.VMEM((n_vars, patches, width), F32),
            pltpu.VMEM((n_vars, 3, patches, H), F32),
            pltpu.VMEM((slots, width), BF16),
            pltpu.VMEM((var_local, 1, D), F32),
            pltpu.VMEM((n_vars, SUB, D), F32),
            pltpu.VMEM((n_rows, tiles, SUB, LANE), F32),
            pltpu.VMEM((n_rows, tiles, SUB, LANE), F32),
            pltpu.VMEM((n_rows, SUB, LANE), F32),
            pltpu.VMEM((n_rows, SUB, LANE), F32),
            pltpu.VMEM((n_rows, tiles + 1, SUB, LANE), F32),
        ]
        + [row_sem] * 2 + [var_sem] * 6 + [row_sem] * 2 + [var_sem] * 2 + [row_sem] * 6,
        compiler_params=pltpu.CompilerParams(
            collective_id=0, has_side_effects=True, vmem_limit_bytes=48 * 1024 * 1024
        ),
        name="encoder",
    )(
        fields,
        stencil.T,
        stencil_weight.T,
        owner_map,
        owner_map.reshape(1, patches),
        embed_weight.reshape(vp, D),
        embed_bias.astype(F32),
        agg_query.reshape(1, D),
        out_grad,
    )
    if depth != slot_depth:
        tokens = tokens.reshape(n_rows, depth, width)[:, :slot_depth].reshape(capacity, width)
    return (
        tokens,
        field_grad,
        weight_grad.reshape(var_local, P_SIZE, D),
        bias_grad,
        query_grad[0].reshape(H, DH),
    )


def solution(mesh):
    return jax.shard_map(
        local,
        mesh=mesh,
        in_specs=(
            P("vars", "rows"),
            P("rows", None),
            P("rows", None),
            P("rows", None),
            P("vars", None, None),
            P("vars", None),
            P(),
            P("rows", None),
        ),
        out_specs=(
            P("rows", "vars"),
            P("vars", "rows"),
            P("vars", None, None),
            P("vars", None),
            P(),
        ),
        check_vma=False,
    )
```

time: 241 us -> 69.6 us (0.29)
  the two profiles are of different devices: /device:TPU:0 before, /device:TPU:12 now
where the time goes in v1:
time: 69.6 us; the launch traced here: 69.3 us
  Pallas kernels  60.9 us (88%)
  local copies, waits for them, and re-layouts  7.02 us (10%)
  other arithmetic  0.72 us (1%)
    pallas_call x1, Pallas kernels, local(): pl.pallas_call(functools.partial(kernel, n_rows, n_vars, var_local, block...  60.9 us
    unnamed x17, local copies, waits for them, and re-layouts  5.53 us

profile of v1, /device:TPU:12, one launch (start us, length us, event | category | flops | bytes accessed | tf_op | source)
XLA Modules:
  0.0 69.3 jit_solution(5416236605557358581)
XLA Ops:
  0.6 0.0 copy-start.5
  0.6 0.0 copy-start.2
  0.7 0.8 %reshape.24.query = f32[1,1024]{1,0:T(1,128)S(1)} reshape(f32[16,64]{1,0:T(8,128)} %param.14) | data formatting | bytes 8192 | tf_op jit(solution)/shard_map/reshape | solution.py:443
  1.5 0.7 %convert_element_type.3.bias = f32[8,1024]{1,0:T(8,128)S(1)} convert(bf16[8,1024]{1,0:T(8,128)(2,1)} %param.13) | non-fusion elementwise | flops 8192 | bytes 49152 | tf_op jit(solution)/shard_map/convert_element_type | solution.py:442
  2.2 0.0 copy-done.5
  2.2 0.0 copy-start.3
  2.2 0.0 copy-start.4
  2.2 0.1 copy.13.owner_col
  2.3 0.0 copy-done.2
  2.3 0.6 copy-done.3
  2.9 0.0 copy-done.4
  3.0 0.0 copy-start
  3.0 1.0 %copy-done = bf16[256,1024]{1,0:T(8,128)(2,1)S(1)} copy-done((bf16[256,1024]{1,0:T(8,128)(2,1)S(1)}, bf16[256,1024]{1,0:T(8,128)(2,1)}, u32[]{:S(2)}) %copy-start) | copy-done | bytes 524312
  4.0 0.0 copy-start.1
  4.0 0.9 %copy-done.1 = bf16[8,16,1024]{2,1,0:T(8,128)(2,1)S(1)} copy-done((bf16[8,16,1024]{2,1,0:T(8,128)(2,1)S(1)}, bf16[8,16,1024]{2,1,0:T(8,128)(2,1)}, u32[]{:S(2)}) %copy-start.1) | copy-done | bytes 262168
  4.9 60.9 %encoder.1 = (bf16[256,512]{1,0:T(8,128)(2,1)S(1)}, f32[8,4096]{1,0:T(8,128)S(1)}, f32[128,1024]{1,0:T(8,128)S(1)}, f32[8,1024]{1,0:T(8,128)S(1)}, f32[8,1024]{1,0:T(8,128)S(1)}) custom-call(bf16[8,4096]{1,0:T(8,128)(2,1)S(1)} %copy-done.2, s32[4,2048]{1,0:T(4,128)S(1)} %bitcast.7, f32[4,2048]{1,0:T(4,128)S(1)} %bitcast.8, s32[128,1]{1,0:T(8,128)S(1)} %copy.13.owner_col, ...), custom_call_target="tpu_custom_call" | custom-call | tf_op jit(solution)/shard_map/encoder/pallas_call | solution.py:398
  65.8 0.7 reshape_squeeze.3
  66.5 0.7 %copy.18 = bf16[256,512]{1,0:T(8,128)(2,1)} copy(bf16[256,512]{1,0:T(8,128)(2,1)S(1)} %get-tuple-element.20) | data formatting | bytes 524288
  67.2 0.7 copy.19
  67.9 0.8 %copy.20 = f32[8,16,1024]{2,1,0:T(8,128)} copy(f32[8,16,1024]{2,1,0:T(8,128)S(1)} %bitcast.5) | data formatting | bytes 1048576
  68.7 0.6 copy.21
  (1 shorter events, 0.0 us)
Async XLA Ops:
  0.6 1.6 %copy-start.5 = (s32[128,1]{0,1:T(1,128)S(1)}, s32[128,1]{0,1:T(1,128)}, u32[]{:S(2)}) copy-start(s32[128,1]{0,1:T(1,128)} %param.11) | copy-start | bytes 1540
  0.6 1.7 %copy-start.2 = (bf16[8,4096]{1,0:T(8,128)(2,1)S(1)}, bf16[8,4096]{1,0:T(8,128)(2,1)}, u32[]{:S(2)}) copy-start(bf16[8,4096]{1,0:T(8,128)(2,1)} %fields.1) | copy-start | bytes 196612
  2.2 0.8 %copy-start.3 = (s32[2048,4]{0,1:T(4,128)S(1)}, s32[2048,4]{0,1:T(4,128)}, u32[]{:S(2)}) copy-start(s32[2048,4]{0,1:T(4,128)} %param.9) | copy-start | bytes 98308
  2.2 0.8 %copy-start.4 = (f32[2048,4]{0,1:T(4,128)S(1)}, f32[2048,4]{0,1:T(4,128)}, u32[]{:S(2)}) copy-start(f32[2048,4]{0,1:T(4,128)} %param.10) | copy-start | bytes 98308
  3.0 1.0 %copy-start = (bf16[256,1024]{1,0:T(8,128)(2,1)S(1)}, bf16[256,1024]{1,0:T(8,128)(2,1)}, u32[]{:S(2)}) copy-start(bf16[256,1024]{1,0:T(8,128)(2,1)} %out_grad.1) | copy-start | bytes 1572868
  4.0 0.9 %copy-start.1 = (bf16[8,16,1024]{2,1,0:T(8,128)(2,1)S(1)}, bf16[8,16,1024]{2,1,0:T(8,128)(2,1)}, u32[]{:S(2)}) copy-start(bf16[8,16,1024]{2,1,0:T(8,128)(2,1)} %param.12) | copy-start | bytes 786436

commit v2 on v1

--- a/solution.py
+++ b/solution.py
@@ -18,6 +18,9 @@
 LANE = 128
 SUB = 8
 J_STEP = 64
+PLANE = 4
+PAIR = 2
+COPIES = 2 * H
 MESH = pl.DeviceIdType.MESH
 F32 = jnp.float32
 BF16 = jnp.bfloat16
@@ -41,8 +44,8 @@
 
 
 def expand(x, spread):
-    high, low = split_two(x)
-    return nn(high, spread) + nn(low, spread)
+    high = x.astype(BF16).astype(F32)
+    return nn(jnp.where(iota(x.shape, 1) < H, high, x - high).astype(BF16), spread)
 
 
 def aligned(start, size):
@@ -52,15 +55,17 @@
 def kernel(
     n_rows, n_vars, var_local, blocks, depth,
     fields, stencil, stencil_weight, owner_col, owner_row, weight, bias, query, out_grad,
-    tok_out, field_out, weight_out, bias_out, query_out,
-    arrived, matrix, spread_fields, up, pix_t, emb, scores, attn_grad,
+    tok_out, field_out, done,
+    weight_in, arrived, matrix, spread_fields, up, pix_t, emb, bias_wide, scores, attn_grad,
     mix_send, mix_recv, stat, tok_send, bias_sum, query_part, part_send, part_recv,
-    small_send, small_recv, done,
+    small_send, small_recv, plane_sum, line_recv,
     og_s, og_r, sw_s, sw_r, mx_s, mx_r, st_s, st_r, tk_s, tk_r, qp_s, qp_r,
-    pt_s, pt_r, sm_s, sm_r, dn_s, dn_r,
+    pt_s, pt_r, sm_s, sm_r, ln_s, ln_r, up_s, up_r, dn_s, dn_r, load_sem,
 ):
     me = lax.axis_index("rows")
     mine = lax.axis_index("vars")
+    lines = n_rows // PLANE
+    my_line, my_place = me // PLANE, lax.rem(me, PLANE)
     patches = blocks * PB
     vp = var_local * P_SIZE
     width = D // n_vars
@@ -92,6 +97,23 @@
         for i in range(1, n_vars):
             body(lax.rem(mine + i, n_vars))
 
+    def each_place(body):
+        for i in range(1, PLANE):
+            body(lax.rem(my_place + i, PLANE))
+
+    def each_line(body):
+        for i in range(1, lines):
+            body(lax.rem(my_line + i, lines))
+
+    own_lanes = pl.ds(pl.multiple_of(mine * width, LANE), width)
+    weight_load = pltpu.make_async_copy(weight, weight_in, load_sem.at[0])
+    weight_load.start()
+    own_load = pltpu.make_async_copy(
+        out_grad.at[aligned(me, depth), own_lanes],
+        arrived.at[mine, aligned(me, depth), :],
+        load_sem.at[1],
+    )
+    own_load.start()
     barrier = pltpu.get_barrier_semaphore()
     each_row(
         lambda p: pl.semaphore_signal(barrier, inc=1, device_id=row_dev(p), device_id_type=MESH)
@@ -101,8 +123,6 @@
     )
     pl.semaphore_wait(barrier, n_rows + n_vars - 2)
 
-    own_lanes = pl.ds(pl.multiple_of(mine * width, LANE), width)
-
     def og_copy(src_row, dst_row, send, recv, p):
         return copy(
             out_grad.at[aligned(src_row, depth), own_lanes],
@@ -111,7 +131,6 @@
         )
 
     each_row(lambda p: og_copy(p, me, p, me, p).start())
-    arrived[mine, aligned(me, depth), :] = out_grad[aligned(me, depth), own_lanes]
 
     def own_pixel(shape, row_axis):
         return iota(shape, 0) % P_SIZE == iota(shape, 1) % P_SIZE
@@ -163,6 +182,7 @@
     take = (slot_col == iota((patches, slots), 1)).astype(F32).astype(BF16)
     put = (slot_row == iota((slots, patches), 0)).astype(F32).astype(BF16)
 
+    own_load.wait()
     each_row(lambda p: og_copy(p, p, p, p, p).wait_recv())
 
     def swap_copy(part, sem_s, sem_r, p):
@@ -170,44 +190,63 @@
 
     each_var(lambda p: swap_copy(mine, p, mine, p).start())
 
-    heads = iota((H, D), 0) == iota((H, D), 1) // DH
+    heads = iota((COPIES, D), 0) % H == iota((COPIES, D), 1) // DH
     spread = heads.astype(F32).astype(BF16)
-    own_heads = iota((H, width), 0) == (mine * width + iota((H, width), 1)) // DH
-    own_spread = own_heads.astype(F32).astype(BF16)
-    query_wide = jnp.where(heads, query[...], 0.0)
-    query_a = query_wide.astype(BF16)
-    rest = query_wide - query_a.astype(F32)
-    query_b = rest.astype(BF16)
-    query_c = (rest - query_b.astype(F32)).astype(BF16)
-
-    def embed(v, carry):
-        mask = iota((patches, vp), 1) // P_SIZE == v
-        own = jnp.where(mask, pix, 0.0).astype(BF16)
-        low = (nn(own, weight[...]) + bias[pl.ds(v, 1), :]).astype(BF16)
-        emb[v] = low
-        scores[v] = (nt(low, query_a) + nt(low, query_b) + nt(low, query_c)) * scale
+    own_head = (mine * width + iota((COPIES, width), 1)) // DH
+    own_spread = (iota((COPIES, width), 0) % H == own_head).astype(F32).astype(BF16)
+    query_tiled = jnp.concatenate([query[...]] * H, axis=1)
+    query_wide = jnp.where(heads, jnp.concatenate([query_tiled] * 2, axis=0), 0.0)
+    query_scaled = jnp.sum(query_wide[:H], axis=0, keepdims=True) * scale
+    query_a = query_wide.astype(BF16).astype(F32)
+    query_b = (query_wide - query_a).astype(BF16).astype(F32)
+    query_c = query_wide - query_a - query_b
+    query_all_parts = jnp.concatenate([query_a, query_b, query_c], axis=0).astype(BF16)
+    bias_wide[...] = bias[...].astype(F32).reshape(var_local, 1, D)
+    pair_shape = (PAIR, patches, vp)
+    pair_rows = PAIR * patches
+    weight_load.wait()
+
+    def pair_mask(g):
+        return PAIR * g + iota(pair_shape, 0) == iota(pair_shape, 2) // P_SIZE
+
+    def embed(g, carry):
+        own = jnp.where(pair_mask(g), pix[None], 0.0).reshape(pair_rows, vp).astype(BF16)
+        pair = pl.ds(PAIR * g, PAIR)
+        projected = nn(own, weight_in[...]).reshape(PAIR, patches, D)
+        low = (projected + bias_wide[pair]).astype(BF16)
+        emb[pair] = low
+        parts = nt(low.reshape(pair_rows, D), query_all_parts)
+        scores[pair] = (
+            (parts[:, :COPIES] + parts[:, COPIES : 2 * COPIES] + parts[:, 2 * COPIES :]) * scale
+        ).reshape(PAIR, patches, COPIES)
         return carry
 
-    lax.fori_loop(0, var_local, embed, 0)
+    lax.fori_loop(0, var_local // PAIR, embed, 0)
     each_var(lambda p: swap_copy(p, p, p, p).wait_recv())
     for part in range(n_vars):
         up[:, part * width : (part + 1) * width] = nn(take, arrived[part])
 
     peak = jnp.max(scores[...], axis=0)
 
-    def gather(v, carry):
+    def gather(g, carry):
         total, inner, mixed = carry
-        values = emb[v].astype(F32)
-        high, low = split_two(up[...] * values)
-        grad = nt(high, spread) + nt(low, spread)
-        attn_grad[v] = grad
-        power = jnp.exp(scores[v] - peak)
-        scores[v] = power
-        return total + power, inner + power * grad, mixed + expand(power, spread) * values
-
-    nothing = jnp.zeros((patches, H), F32)
+        pair = pl.ds(PAIR * g, PAIR)
+        values = emb[pair].astype(F32)
+        high, low = split_two((up[...][None] * values).reshape(pair_rows, D))
+        grad = (nt(high, spread) + nt(low, spread)).reshape(PAIR, patches, COPIES)
+        attn_grad[pair] = grad
+        power = jnp.exp(scores[pair] - peak[None])
+        scores[pair] = power
+        wide = expand(power.reshape(pair_rows, COPIES), spread).reshape(PAIR, patches, D)
+        return (
+            total + jnp.sum(power, axis=0),
+            inner + jnp.sum(power * grad, axis=0),
+            mixed + jnp.sum(wide * values, axis=0),
+        )
+
+    nothing = jnp.zeros((patches, COPIES), F32)
     total, inner, mixed = lax.fori_loop(
-        0, var_local, gather, (nothing, nothing, jnp.zeros((patches, D), F32))
+        0, var_local // PAIR, gather, (nothing, nothing, jnp.zeros((patches, D), F32))
     )
     stat[mine, 0] = peak
     stat[mine, 1] = total
@@ -250,49 +289,60 @@
     each_row(lambda p: tok_copy(p, me, p, me, p).start())
     tok_out[aligned(me, depth), :] = tok_send[aligned(me, depth), :]
 
-    query_scaled = query[...] * scale
-
-    def part_copy(slot_s, slot_r, send, recv, p):
-        return copy(
-            part_send.at[slot_s], part_recv.at[slot_r], pt_s.at[send], pt_r.at[recv], row_dev(p)
+    def part_copy(slot, from_place, line, to_place):
+        return copy(
+            part_send.at[slot], part_recv.at[from_place, line],
+            pt_s.at[slot], pt_r.at[from_place, line], row_dev(my_line * PLANE + to_place),
         )
 
     per_group = D // LANE // tiles
-    per_var = P_SIZE // SUB * per_group
+    per_pair = PAIR * P_SIZE // SUB * per_group
+    pair_pixels = PAIR * P_SIZE
 
     def backward(i, carry):
         pix_grad, query_sum = carry
-        v = lax.rem(i + me // per_var, var_local)
-        values = emb[v].astype(F32)
-        attention = scores[v] * own_factor
-        score_grad = attention * (attn_grad[v] - inner_all)
-        score_wide = expand(score_grad, spread)
-        grad = expand(attention, spread) * up[...] + score_wide * query_scaled
-        low = grad.astype(BF16)
-        bias_sum[v] = jnp.sum(grad, axis=0, keepdims=True)
-        query_sum = query_sum + jnp.sum(score_wide * values, axis=0, keepdims=True)
-        found = nn(pix_t[aligned(v, P_SIZE), :], low)
-        for group in range(P_SIZE // SUB):
+        g = lax.rem(i + my_line + 1, var_local // PAIR)
+        pair = pl.ds(PAIR * g, PAIR)
+        values = emb[pair].astype(F32)
+        attention = scores[pair] * own_factor[None]
+        score_grad = attention * (attn_grad[pair] - inner_all[None])
+        both = jnp.concatenate(
+            [attention.reshape(pair_rows, COPIES), score_grad.reshape(pair_rows, COPIES)], axis=0
+        )
+        wide = expand(both, spread)
+        attention_wide = wide[:pair_rows].reshape(PAIR, patches, D)
+        score_wide = wide[pair_rows:].reshape(PAIR, patches, D)
+        grad = attention_wide * up[...][None] + score_wide * query_scaled[None]
+        low = grad.astype(BF16).reshape(pair_rows, D)
+        bias_sum[pair] = jnp.sum(grad, axis=1, keepdims=True)
+        query_sum = query_sum + jnp.sum(jnp.sum(score_wide * values, axis=0), axis=0, keepdims=True)
+        rows = pix_t[aligned(g, pair_pixels), :].astype(F32)
+        doubled = jnp.concatenate([rows] * PAIR, axis=1)
+        kept = iota(doubled.shape, 0) // P_SIZE == iota(doubled.shape, 1) // patches
+        found = nn(jnp.where(kept, doubled, 0.0).astype(BF16), low)
+        for group in range(pair_pixels // SUB):
             for lane in range(D // LANE):
-                slot = v * per_var + group * per_group + lane // tiles
+                slot = g * per_pair + group * per_group + lane // tiles
                 part_send[slot, lane % tiles] = found[
                     group * SUB : (group + 1) * SUB, lane * LANE : (lane + 1) * LANE
                 ]
-        for step in range(per_var):
-            slot = v * per_var + step
-
-            @pl.when(slot != me)
+        for step in range(per_pair):
+            slot = g * per_pair + step
+            place = lax.rem(slot, PLANE)
+
+            @pl.when(place != my_place)
             def _():
-                part_copy(slot, me, slot, me, slot).start()
-
-        mask = iota((patches, vp), 1) // P_SIZE == v
-        pix_grad = pix_grad + jnp.where(mask, nt(low, weight[...]), 0.0)
+                part_copy(slot, my_place, slot // PLANE, place).start()
+
+        returned = nt(low, weight_in[...]).reshape(pair_shape)
+        pix_grad = pix_grad + jnp.sum(jnp.where(pair_mask(g), returned, 0.0), axis=0)
         return pix_grad, query_sum
 
     pix_grad, query_sum = lax.fori_loop(
-        0, var_local, backward, (jnp.zeros((patches, vp), F32), jnp.zeros((1, D), F32))
-    )
-    part_recv[me] = part_send[me]
+        0, var_local // PAIR, backward, (jnp.zeros((patches, vp), F32), jnp.zeros((1, D), F32))
+    )
+    for line in range(lines):
+        part_recv[my_place, line] = part_send[line * PLANE + my_place]
 
     query_part[mine] = jnp.broadcast_to(query_sum * scale, (SUB, D))
 
@@ -311,21 +361,24 @@
     for group in range(var_local // SUB):
         rows = jnp.concatenate([bias_sum[group * SUB + k] for k in range(SUB)], axis=0)
         for lane in range(D // LANE):
-            small_send[group * (D // LANE) + lane] = rows[:, lane * LANE : (lane + 1) * LANE]
+            number = group * (D // LANE) + lane
+            small_send[number % PLANE, number // PLANE] = rows[:, lane * LANE : (lane + 1) * LANE]
     each_var(lambda p: query_copy(p, p, p, p).wait_recv())
     query_all = query_part[0]
     for part in range(1, n_vars):
         query_all = query_all + query_part[part]
     for lane in range(D // LANE):
-        small_send[bias_tiles + lane] = query_all[:, lane * LANE : (lane + 1) * LANE]
-
-    def small_copy(slot_s, slot_r, send, recv, p):
-        return copy(
-            small_send.at[slot_s], small_recv.at[slot_r], sm_s.at[send], sm_r.at[recv], row_dev(p)
-        )
-
-    each_row(lambda p: small_copy(p, me, p, me, p).start())
-    small_recv[me] = small_send[me]
+        number = bias_tiles + lane
+        small_send[number % PLANE, number // PLANE] = query_all[:, lane * LANE : (lane + 1) * LANE]
+
+    def small_copy(to_place, from_place, send, recv, p):
+        return copy(
+            small_send.at[to_place], small_recv.at[from_place], sm_s.at[send], sm_r.at[recv],
+            row_dev(my_line * PLANE + p),
+        )
+
+    each_place(lambda p: small_copy(p, my_place, p, my_place, p).start())
+    small_recv[my_place] = small_send[my_place]
 
     def field_block(b, carry):
         values = nn(grad_t, placing(b))
@@ -336,41 +389,95 @@
 
     lax.fori_loop(0, blocks, field_block, 0)
 
-    each_row(lambda p: part_copy(p, p, p, p, p).wait_recv())
-    each_row(lambda p: small_copy(p, p, p, p, p).wait_recv())
-    done[me, 0:tiles] = jnp.sum(part_recv[...], axis=0)
-    done[me, tiles] = jnp.sum(small_recv[...], axis=0)
-
-    def done_copy(slot, send, recv, p):
-        return copy(done.at[slot], done.at[slot], dn_s.at[send], dn_r.at[recv], row_dev(p))
-
-    each_row(lambda p: done_copy(me, p, me, p).start())
-    each_row(lambda p: done_copy(p, p, p, p).wait_recv())
-    for slot in range(n_rows):
-        for tile in range(tiles):
-            number = slot * tiles + tile
-            group, lane = number // (D // LANE), number % (D // LANE)
-            weight_out[group * SUB : (group + 1) * SUB, lane * LANE : (lane + 1) * LANE] = done[
-                slot, tile
-            ]
-    for number in range(bias_tiles):
-        group, lane = number // (D // LANE), number % (D // LANE)
-        bias_out[group * SUB : (group + 1) * SUB, lane * LANE : (lane + 1) * LANE] = done[
-            number, tiles
-        ]
-    for lane in range(D // LANE):
-        query_out[:, lane * LANE : (lane + 1) * LANE] = done[bias_tiles + lane, tiles]
+    each_place(lambda p: small_copy(p, p, p, p, p).wait_recv())
+
+    def line_copy(to_line, from_line, p):
+        return copy(
+            plane_sum.at[to_line], line_recv.at[from_line], ln_s.at[to_line], ln_r.at[from_line],
+            row_dev(p * PLANE + my_place),
+        )
+
+    def plane_total(line):
+        each_place(lambda p: part_copy(p, p, line, p).wait_recv())
+        part_total, small_total = part_recv[0, line], small_recv[0, line]
+        for place in range(1, PLANE):
+            part_total = part_total + part_recv[place, line]
+            small_total = small_total + small_recv[place, line]
+        plane_sum[line, 0:tiles] = part_total
+        plane_sum[line, tiles] = small_total
+
+    def send_line(line):
+        plane_total(line)
+        line_copy(line, my_line, line).start()
+
+    each_line(send_line)
+    plane_total(my_line)
+    line_recv[my_line] = plane_sum[my_line]
+    each_line(lambda p: line_copy(p, p, p).wait_recv())
+    done[my_line, my_place] = jnp.sum(line_recv[...], axis=0)
+
+    def up_copy(line, send, recv, p):
+        return copy(
+            done.at[line, my_place], done.at[line, my_place], up_s.at[send], up_r.at[recv],
+            row_dev(p * PLANE + my_place),
+        )
+
+    def done_copy(line, place, to_place):
+        return copy(
+            done.at[line, place], done.at[line, place], dn_s.at[line, to_place],
+            dn_r.at[line, place], row_dev(my_line * PLANE + to_place),
+        )
+
+    each_line(lambda p: up_copy(my_line, p, my_line, p).start())
+    each_place(lambda p: done_copy(my_line, my_place, p).start())
+
+    def pass_on(line):
+        up_copy(line, line, line, line).wait_recv()
+        each_place(lambda p: done_copy(line, my_place, p).start())
+
+    each_line(pass_on)
+    for line in range(lines):
+        each_place(lambda p: done_copy(line, p, p).wait_recv())
 
     each_row(lambda p: tok_copy(p, p, p, p, p).wait_recv())
     each_row(lambda p: og_copy(p, me, p, me, p).wait_send())
     each_row(lambda p: tok_copy(p, me, p, me, p).wait_send())
-    each_row(lambda p: part_copy(p, me, p, me, p).wait_send())
-    each_row(lambda p: small_copy(p, me, p, me, p).wait_send())
-    each_row(lambda p: done_copy(me, p, me, p).wait_send())
+    for line in range(lines):
+        each_place(lambda p: part_copy(line * PLANE + p, my_place, line, p).wait_send())
+        each_place(lambda p: done_copy(line, my_place, p).wait_send())
+    each_place(lambda p: small_copy(p, my_place, p, my_place, p).wait_send())
+    each_line(lambda p: line_copy(p, my_line, p).wait_send())
+    each_line(lambda p: up_copy(my_line, p, my_line, p).wait_send())
     each_var(lambda p: swap_copy(mine, p, mine, p).wait_send())
     each_var(lambda p: stat_copy(mine, p, mine, p).wait_send())
     each_var(lambda p: mix_copy(p, mine, p, mine, p).wait_send())
     each_var(lambda p: query_copy(mine, p, mine, p).wait_send())
+
+
+def finish(
+    n_rows, tiles, bias_tiles, tok_in, field_in, done,
+    tok_out, field_out, weight_out, bias_out, query_out,
+):
+    tok_out[...] = tok_in[...]
+    field_out[...] = field_in[...]
+    across = D // LANE
+    for number in range(n_rows * tiles):
+        slot, tile = number // tiles, number % tiles
+        group, lane = number // across, number % across
+        weight_out[group * SUB : (group + 1) * SUB, lane * LANE : (lane + 1) * LANE] = done[
+            slot // PLANE, slot % PLANE, tile
+        ]
+    for number in range(bias_tiles):
+        group, lane = number // across, number % across
+        bias_out[group * SUB : (group + 1) * SUB, lane * LANE : (lane + 1) * LANE] = done[
+            number // PLANE, number % PLANE, tiles
+        ]
+    for lane in range(across):
+        number = bias_tiles + lane
+        row = done[number // PLANE, number % PLANE, tiles]
+        for half in range(LANE // DH):
+            head = lane * (LANE // DH) + half
+            query_out[head : head + 1, :] = row[0:1, half * DH : (half + 1) * DH]
 
 
 def local(
@@ -395,41 +502,47 @@
     vmem = pl.BlockSpec(memory_space=pltpu.VMEM)
     dma = pltpu.SemaphoreType.DMA
     row_sem, var_sem = dma((n_rows,)), dma((n_vars,))
-    tokens, field_grad, weight_grad, bias_grad, query_grad = pl.pallas_call(
+    lines = n_rows // PLANE
+    shapes = (
+        jax.ShapeDtypeStruct((slots, width), BF16),
+        jax.ShapeDtypeStruct((var_local, points), F32),
+    )
+    tokens, field_grad, done = pl.pallas_call(
         functools.partial(kernel, n_rows, n_vars, var_local, blocks, depth),
-        out_shape=(
-            jax.ShapeDtypeStruct((slots, width), BF16),
-            jax.ShapeDtypeStruct((var_local, points), F32),
-            jax.ShapeDtypeStruct((vp, D), F32),
-            jax.ShapeDtypeStruct((var_local, D), F32),
-            jax.ShapeDtypeStruct((SUB, D), F32),
-        ),
-        in_specs=[vmem] * 9,
-        out_specs=(vmem,) * 5,
+        out_shape=shapes
+        + (jax.ShapeDtypeStruct((lines, PLANE, tiles + 1, SUB, LANE), F32),),
+        in_specs=[vmem] * 5 + [pl.BlockSpec(memory_space=pl.ANY)] + [vmem] * 2
+        + [pl.BlockSpec(memory_space=pl.ANY)],
+        out_specs=(vmem,) * 3,
         scratch_shapes=[
+            pltpu.VMEM((vp, D), BF16),
             pltpu.VMEM((n_vars, slots, width), BF16),
             pltpu.VMEM((blocks, PTS_BLK, PB * P_SIZE), BF16),
             pltpu.VMEM((vp, PTS_BLK), BF16),
             pltpu.VMEM((patches, D), F32),
             pltpu.VMEM((vp, patches), BF16),
             pltpu.VMEM((var_local, patches, D), BF16),
-            pltpu.VMEM((var_local, patches, H), F32),
-            pltpu.VMEM((var_local, patches, H), F32),
+            pltpu.VMEM((var_local, 1, D), F32),
+            pltpu.VMEM((var_local, patches, COPIES), F32),
+            pltpu.VMEM((var_local, patches, COPIES), F32),
             pltpu.VMEM((n_vars, patches, width), F32),
             pltpu.VMEM((n_vars, patches, width), F32),
-            pltpu.VMEM((n_vars, 3, patches, H), F32),
+            pltpu.VMEM((n_vars, 3, patches, COPIES), F32),
             pltpu.VMEM((slots, width), BF16),
             pltpu.VMEM((var_local, 1, D), F32),
             pltpu.VMEM((n_vars, SUB, D), F32),
             pltpu.VMEM((n_rows, tiles, SUB, LANE), F32),
-            pltpu.VMEM((n_rows, tiles, SUB, LANE), F32),
-            pltpu.VMEM((n_rows, SUB, LANE), F32),
-            pltpu.VMEM((n_rows, SUB, LANE), F32),
-            pltpu.VMEM((n_rows, tiles + 1, SUB, LANE), F32),
+            pltpu.VMEM((PLANE, lines, tiles, SUB, LANE), F32),
+            pltpu.VMEM((PLANE, lines, SUB, LANE), F32),
+            pltpu.VMEM((PLANE, lines, SUB, LANE), F32),
+            pltpu.VMEM((lines, tiles + 1, SUB, LANE), F32),
+            pltpu.VMEM((lines, tiles + 1, SUB, LANE), F32),
         ]
-        + [row_sem] * 2 + [var_sem] * 6 + [row_sem] * 2 + [var_sem] * 2 + [row_sem] * 6,
+        + [row_sem] * 2 + [var_sem] * 6 + [row_sem] * 2 + [var_sem] * 2
+        + [row_sem, dma((PLANE, lines))] + [dma((PLANE,))] * 2 + [dma((lines,))] * 4
+        + [dma((lines, PLANE))] * 2 + [dma((2,))],
         compiler_params=pltpu.CompilerParams(
-            collective_id=0, has_side_effects=True, vmem_limit_bytes=48 * 1024 * 1024
+            collective_id=0, has_side_effects=True, vmem_limit_bytes=56 * 1024 * 1024
         ),
         name="encoder",
     )(
@@ -439,19 +552,26 @@
         owner_map,
         owner_map.reshape(1, patches),
         embed_weight.reshape(vp, D),
-        embed_bias.astype(F32),
-        agg_query.reshape(1, D),
+        embed_bias,
+        agg_query,
         out_grad,
     )
+    tokens, field_grad, weight_grad, bias_grad, query_grad = pl.pallas_call(
+        functools.partial(finish, n_rows, tiles, var_local // SUB * (D // LANE)),
+        out_shape=shapes
+        + (
+            jax.ShapeDtypeStruct((vp, D), F32),
+            jax.ShapeDtypeStruct((var_local, D), F32),
+            jax.ShapeDtypeStruct((H, DH), F32),
+        ),
+        in_specs=[vmem] * 3,
+        out_specs=(vmem,) * 5,
+        compiler_params=pltpu.CompilerParams(vmem_limit_bytes=32 * 1024 * 1024),
+        name="finish",
+    )(tokens, field_grad, done)
     if depth != slot_depth:
         tokens = tokens.reshape(n_rows, depth, width)[:, :slot_depth].reshape(capacity, width)
-    return (
-        tokens,
-        field_grad,
-        weight_grad.reshape(var_local, P_SIZE, D),
-        bias_grad,
-        query_grad[0].reshape(H, DH),
-    )
+    return tokens, field_grad, weight_grad.reshape(var_local, P_SIZE, D), bias_grad, query_grad
 
 
 def solution(mesh):

time: 69.6 us -> 55.8 us (0.80)
  the two profiles are of different devices: /device:TPU:12 before, /device:TPU:0 now
where the time goes in v2:
time: 55.8 us; the launch traced here: 55.6 us
  Pallas kernels  50.6 us (91%)
  local copies, waits for them, and re-layouts  4.3 us (8%)
  between operations  0.66 us (1%)
    pallas_call x1, Pallas kernels, local(): pl.pallas_call(functools.partial(kernel, n_rows, n_vars, var_local, block...  49.7 us
    unnamed x9, local copies, waits for them, and re-layouts  4.3 us

profile of v2, /device:TPU:0, one launch (start us, length us, event | category | flops | bytes accessed | tf_op | source)
XLA Modules:
  0.0 55.6 jit_solution(12940631488266776076)
XLA Ops:
  0.6 0.0 copy-start.3
  0.6 0.6 %copy-done.3 = s32[128,1]{0,1:T(1,128)S(1)} copy-done((s32[128,1]{0,1:T(1,128)S(1)}, s32[128,1]{0,1:T(1,128)}, u32[]{:S(2)}) %copy-start.3) | copy-done | bytes 536
  1.3 0.7 %copy.13.owner_col = s32[128,1]{1,0:T(8,128)} copy(s32[128,1]{0,1:T(1,128)S(1)} %copy-done.3) | data formatting | bytes 1024 | tf_op args[3]
  2.0 49.7 %encoder.1 = (bf16[256,512]{1,0:T(8,128)(2,1)}, f32[8,4096]{1,0:T(8,128)}, f32[4,4,9,8,128]{4,3,2,1,0:T(8,128)}) custom-call(bf16[8,4096]{1,0:T(8,128)(2,1)} %fields.1, s32[4,2048]{1,0:T(4,128)} %bitcast.6, f32[4,2048]{1,0:T(4,128)} %bitcast.7, s32[128,1]{1,0:T(8,128)} %copy.13.owner_col, s32[1,128]{1,0:T(1,128)} %bitcast.8, bf16[128,1024]{1,0:T(8,128)(2,1)} %bitcast.5, ...), custom_call_target="tpu_custom_call" | custom-call | tf_op jit(solution)/shard_map/encoder/pallas_call | solution.py:510
  51.7 0.0 copy-start
  51.7 1.1 %copy-done = f32[4,4,9,8,128]{4,3,2,1,0:T(8,128)S(1)} copy-done((f32[4,4,9,8,128]{4,3,2,1,0:T(8,128)S(1)}, f32[4,4,9,8,128]{4,3,2,1,0:T(8,128)}, u32[]{:S(2)}) %copy-start) | copy-done | bytes 589848
  52.8 0.0 copy-start.1
  52.8 0.9 %copy-done.1 = bf16[256,512]{1,0:T(8,128)(2,1)S(1)} copy-done((bf16[256,512]{1,0:T(8,128)(2,1)S(1)}, bf16[256,512]{1,0:T(8,128)(2,1)}, u32[]{:S(2)}) %copy-start.1) | copy-done | bytes 262168
  53.7 0.0 copy-start.2
  53.7 0.9 %copy-done.2 = f32[8,4096]{1,0:T(8,128)S(1)} copy-done((f32[8,4096]{1,0:T(8,128)S(1)}, f32[8,4096]{1,0:T(8,128)}, u32[]{:S(2)}) %copy-start.2) | copy-done | bytes 131096
  54.6 0.9 %finish.1 = (bf16[256,512]{1,0:T(8,128)(2,1)}, f32[8,4096]{1,0:T(8,128)}, f32[128,1024]{1,0:T(8,128)}, f32[8,1024]{1,0:T(8,128)}, f32[16,64]{1,0:T(8,128)}) custom-call(bf16[256,512]{1,0:T(8,128)(2,1)S(1)} %copy-done.1, f32[8,4096]{1,0:T(8,128)S(1)} %copy-done.2, f32[4,4,9,8,128]{4,3,2,1,0:T(8,128)S(1)} %copy-done), custom_call_target="tpu_custom_call" | custom-call | tf_op jit(solution)/shard_map/finish/pallas_call | solution.py:559
Async XLA Ops:
  0.6 0.7 %copy-start.3 = (s32[128,1]{0,1:T(1,128)S(1)}, s32[128,1]{0,1:T(1,128)}, u32[]{:S(2)}) copy-start(s32[128,1]{0,1:T(1,128)} %param.11) | copy-start | bytes 1540
  51.7 1.1 %copy-start = (f32[4,4,9,8,128]{4,3,2,1,0:T(8,128)S(1)}, f32[4,4,9,8,128]{4,3,2,1,0:T(8,128)}, u32[]{:S(2)}) copy-start(f32[4,4,9,8,128]{4,3,2,1,0:T(8,128)} %get-tuple-element.15.done) | copy-start | bytes 1769476
  52.8 0.9 %copy-start.1 = (bf16[256,512]{1,0:T(8,128)(2,1)S(1)}, bf16[256,512]{1,0:T(8,128)(2,1)}, u32[]{:S(2)}) copy-start(bf16[256,512]{1,0:T(8,128)(2,1)} %get-tuple-element.13.tok_in) | copy-start | bytes 786436
  53.7 0.9 %copy-start.2 = (f32[8,4096]{1,0:T(8,128)S(1)}, f32[8,4096]{1,0:T(8,128)}, u32[]{:S(2)}) copy-start(f32[8,4096]{1,0:T(8,128)} %get-tuple-element.14.field_in) | copy-start | bytes 393220

commit v3 on v2

--- a/solution.py
+++ b/solution.py
@@ -43,9 +43,13 @@
     return high, (x - high.astype(F32)).astype(BF16)
 
 
+def packed(x):
+    high = x.astype(BF16).astype(F32)
+    return jnp.where(iota(x.shape, 1) < H, high, x - high).astype(BF16)
+
+
 def expand(x, spread):
-    high = x.astype(BF16).astype(F32)
-    return nn(jnp.where(iota(x.shape, 1) < H, high, x - high).astype(BF16), spread)
+    return nn(packed(x), spread)
 
 
 def aligned(start, size):
@@ -58,9 +62,9 @@
     tok_out, field_out, done,
     weight_in, arrived, matrix, spread_fields, up, pix_t, emb, bias_wide, scores, attn_grad,
     mix_send, mix_recv, stat, tok_send, bias_sum, query_part, part_send, part_recv,
-    small_send, small_recv, plane_sum, line_recv,
+    small_send, small_recv, plane_sum, line_recv, small_sum, small_line,
     og_s, og_r, sw_s, sw_r, mx_s, mx_r, st_s, st_r, tk_s, tk_r, qp_s, qp_r,
-    pt_s, pt_r, sm_s, sm_r, ln_s, ln_r, up_s, up_r, dn_s, dn_r, load_sem,
+    pt_s, pt_r, sm_s, sm_r, ln_s, ln_r, sl_s, sl_r, up_s, up_r, dn_s, dn_r, load_sem,
 ):
     me = lax.axis_index("rows")
     mine = lax.axis_index("vars")
@@ -121,7 +125,6 @@
     each_var(
         lambda p: pl.semaphore_signal(barrier, inc=1, device_id=var_dev(p), device_id_type=MESH)
     )
-    pl.semaphore_wait(barrier, n_rows + n_vars - 2)
 
     def og_copy(src_row, dst_row, send, recv, p):
         return copy(
@@ -130,7 +133,6 @@
             og_s.at[send], og_r.at[recv], row_dev(p),
         )
 
-    each_row(lambda p: og_copy(p, me, p, me, p).start())
 
     def own_pixel(shape, row_axis):
         return iota(shape, 0) % P_SIZE == iota(shape, 1) % P_SIZE
@@ -166,7 +168,10 @@
         kept = jnp.where(own_pixel((vp, block_pixels), 0), values, 0.0).astype(BF16)
         return pix + nt(placing(b), kept)
 
-    pix = lax.fori_loop(0, blocks, interp, jnp.zeros((patches, vp), F32))
+    pix = interp(0, jnp.zeros((patches, vp), F32))
+    pl.semaphore_wait(barrier, n_rows + n_vars - 2)
+    each_row(lambda p: og_copy(p, me, p, me, p).start())
+    pix = lax.fori_loop(1, blocks, interp, pix)
     pix_t[...] = pix.T.astype(BF16)
 
     square = (patches, patches)
@@ -228,8 +233,8 @@
 
     peak = jnp.max(scores[...], axis=0)
 
-    def gather(g, carry):
-        total, inner, mixed = carry
+    def weigh(g, carry):
+        total, inner = carry
         pair = pl.ds(PAIR * g, PAIR)
         values = emb[pair].astype(F32)
         high, low = split_two((up[...][None] * values).reshape(pair_rows, D))
@@ -237,32 +242,34 @@
         attn_grad[pair] = grad
         power = jnp.exp(scores[pair] - peak[None])
         scores[pair] = power
-        wide = expand(power.reshape(pair_rows, COPIES), spread).reshape(PAIR, patches, D)
-        return (
-            total + jnp.sum(power, axis=0),
-            inner + jnp.sum(power * grad, axis=0),
-            mixed + jnp.sum(wide * values, axis=0),
-        )
+        return total + jnp.sum(power, axis=0), inner + jnp.sum(power * grad, axis=0)
 
     nothing = jnp.zeros((patches, COPIES), F32)
-    total, inner, mixed = lax.fori_loop(
-        0, var_local // PAIR, gather, (nothing, nothing, jnp.zeros((patches, D), F32))
-    )
+    total, inner = lax.fori_loop(0, var_local // PAIR, weigh, (nothing, nothing))
     stat[mine, 0] = peak
     stat[mine, 1] = total
     stat[mine, 2] = inner
+
+    def stat_copy(part, sem_s, sem_r, p):
+        return copy(stat.at[part], stat.at[part], st_s.at[sem_s], st_r.at[sem_r], var_dev(p))
+
+    def mix_copy(part, slot, sem_s, sem_r, p):
+        return copy(
+            mix_send.at[part], mix_recv.at[slot], mx_s.at[sem_s], mx_r.at[sem_r], var_dev(p)
+        )
+
+    each_var(lambda p: stat_copy(mine, p, mine, p).start())
+
+    def mix(g, mixed):
+        pair = pl.ds(PAIR * g, PAIR)
+        wide = expand(scores[pair].reshape(pair_rows, COPIES), spread)
+        return mixed + jnp.sum(
+            wide.reshape(PAIR, patches, D) * emb[pair].astype(F32), axis=0
+        )
+
+    mixed = lax.fori_loop(0, var_local // PAIR, mix, jnp.zeros((patches, D), F32))
     for part in range(n_vars):
         mix_send[part] = mixed[:, part * width : (part + 1) * width]
-
-    def stat_copy(part, sem_s, sem_r, p):
-        return copy(stat.at[part], stat.at[part], st_s.at[sem_s], st_r.at[sem_r], var_dev(p))
-
-    def mix_copy(part, slot, sem_s, sem_r, p):
-        return copy(
-            mix_send.at[part], mix_recv.at[slot], mx_s.at[sem_s], mx_r.at[sem_r], var_dev(p)
-        )
-
-    each_var(lambda p: stat_copy(mine, p, mine, p).start())
     each_var(lambda p: mix_copy(p, mine, p, mine, p).start())
     mix_recv[mine] = mix_send[mine]
     each_var(lambda p: stat_copy(p, p, p, p).wait_recv())
@@ -274,21 +281,6 @@
     inner_all = sum(stat[part, 2] * factors[part] for part in range(n_vars)) / total_all
     own_factor = jnp.exp(peak - peak_all) / total_all
 
-    each_var(lambda p: mix_copy(p, p, p, p, p).wait_recv())
-    mixture = sum(
-        expand(factors[part] / total_all, own_spread) * mix_recv[part] for part in range(n_vars)
-    )
-    tok_send[...] = nn(put, mixture.astype(BF16)).astype(BF16)
-
-    def tok_copy(src_row, dst_row, send, recv, p):
-        return copy(
-            tok_send.at[aligned(src_row, depth), :], tok_out.at[aligned(dst_row, depth), :],
-            tk_s.at[send], tk_r.at[recv], row_dev(p),
-        )
-
-    each_row(lambda p: tok_copy(p, me, p, me, p).start())
-    tok_out[aligned(me, depth), :] = tok_send[aligned(me, depth), :]
-
     def part_copy(slot, from_place, line, to_place):
         return copy(
             part_send.at[slot], part_recv.at[from_place, line],
@@ -299,23 +291,53 @@
     per_pair = PAIR * P_SIZE // SUB * per_group
     pair_pixels = PAIR * P_SIZE
 
+    pair_lines = per_pair // PLANE
+
+    def turn(i):
+        return lax.rem(i + my_line + 1, var_local // PAIR)
+
+    def line_copy(to_line, from_line, p):
+        return copy(
+            plane_sum.at[to_line], line_recv.at[from_line], ln_s.at[to_line], ln_r.at[from_line],
+            row_dev(p * PLANE + my_place),
+        )
+
+    def plane_total(line):
+        each_place(lambda p: part_copy(p, p, line, p).wait_recv())
+        part_total = part_recv[0, line]
+        for place in range(1, PLANE):
+            part_total = part_total + part_recv[place, line]
+        plane_sum[line] = part_total
+
+    def send_lines(i):
+        for k in range(pair_lines):
+            line = turn(i) * pair_lines + k
+
+            @pl.when(line != my_line)
+            def _():
+                plane_total(line)
+                line_copy(line, my_line, line).start()
+
     def backward(i, carry):
         pix_grad, query_sum = carry
-        g = lax.rem(i + my_line + 1, var_local // PAIR)
+        g = turn(i)
         pair = pl.ds(PAIR * g, PAIR)
-        values = emb[pair].astype(F32)
         attention = scores[pair] * own_factor[None]
         score_grad = attention * (attn_grad[pair] - inner_all[None])
         both = jnp.concatenate(
             [attention.reshape(pair_rows, COPIES), score_grad.reshape(pair_rows, COPIES)], axis=0
         )
-        wide = expand(both, spread)
+        both = packed(both)
+        wide = nn(both, spread)
         attention_wide = wide[:pair_rows].reshape(PAIR, patches, D)
         score_wide = wide[pair_rows:].reshape(PAIR, patches, D)
         grad = attention_wide * up[...][None] + score_wide * query_scaled[None]
         low = grad.astype(BF16).reshape(pair_rows, D)
         bias_sum[pair] = jnp.sum(grad, axis=1, keepdims=True)
-        query_sum = query_sum + jnp.sum(jnp.sum(score_wide * values, axis=0), axis=0, keepdims=True)
+        query_sum = query_sum + lax.dot_general(
+            both[pair_rows:], emb[pair].reshape(pair_rows, D), (((0,), (0,)), ((), ())),
+            preferred_element_type=F32,
+        )
         rows = pix_t[aligned(g, pair_pixels), :].astype(F32)
         doubled = jnp.concatenate([rows] * PAIR, axis=1)
         kept = iota(doubled.shape, 0) // P_SIZE == iota(doubled.shape, 1) // patches
@@ -336,14 +358,32 @@
 
         returned = nt(low, weight_in[...]).reshape(pair_shape)
         pix_grad = pix_grad + jnp.sum(jnp.where(pair_mask(g), returned, 0.0), axis=0)
+        for k in range(pair_lines):
+            line = g * pair_lines + k
+            part_recv[my_place, line] = part_send[line * PLANE + my_place]
+
+        if not isinstance(i, int):
+            send_lines(i - 1)
         return pix_grad, query_sum
 
-    pix_grad, query_sum = lax.fori_loop(
-        0, var_local // PAIR, backward, (jnp.zeros((patches, vp), F32), jnp.zeros((1, D), F32))
+    sums = backward(0, (jnp.zeros((patches, vp), F32), jnp.zeros((COPIES, D), F32)))
+    each_var(lambda p: mix_copy(p, p, p, p, p).wait_recv())
+    mixture = sum(
+        expand(factors[part] / total_all, own_spread) * mix_recv[part] for part in range(n_vars)
     )
-    for line in range(lines):
-        part_recv[my_place, line] = part_send[line * PLANE + my_place]
-
+    tok_send[...] = nn(put, mixture.astype(BF16)).astype(BF16)
+
+    def tok_copy(src_row, dst_row, send, recv, p):
+        return copy(
+            tok_send.at[aligned(src_row, depth), :], tok_out.at[aligned(dst_row, depth), :],
+            tk_s.at[send], tk_r.at[recv], row_dev(p),
+        )
+
+    each_row(lambda p: tok_copy(p, me, p, me, p).start())
+    tok_out[aligned(me, depth), :] = tok_send[aligned(me, depth), :]
+
+    pix_grad, query_rows = lax.fori_loop(1, var_local // PAIR, backward, sums)
+    query_sum = jnp.sum(jnp.where(heads, query_rows, 0.0), axis=0, keepdims=True)
     query_part[mine] = jnp.broadcast_to(query_sum * scale, (SUB, D))
 
     def query_copy(part, sem_s, sem_r, p):
@@ -387,34 +427,26 @@
         field_out[:, aligned(b, PTS_BLK)] = nt(by_pixel, matrix[b])
         return carry
 
-    lax.fori_loop(0, blocks, field_block, 0)
-
-    each_place(lambda p: small_copy(p, p, p, p, p).wait_recv())
-
-    def line_copy(to_line, from_line, p):
-        return copy(
-            plane_sum.at[to_line], line_recv.at[from_line], ln_s.at[to_line], ln_r.at[from_line],
-            row_dev(p * PLANE + my_place),
-        )
-
-    def plane_total(line):
-        each_place(lambda p: part_copy(p, p, line, p).wait_recv())
-        part_total, small_total = part_recv[0, line], small_recv[0, line]
-        for place in range(1, PLANE):
-            part_total = part_total + part_recv[place, line]
-            small_total = small_total + small_recv[place, line]
-        plane_sum[line, 0:tiles] = part_total
-        plane_sum[line, tiles] = small_total
-
-    def send_line(line):
-        plane_total(line)
-        line_copy(line, my_line, line).start()
-
-    each_line(send_line)
+    send_lines(var_local // PAIR - 1)
     plane_total(my_line)
     line_recv[my_line] = plane_sum[my_line]
+    lax.fori_loop(0, blocks // 2, field_block, 0)
+    each_place(lambda p: small_copy(p, p, p, p, p).wait_recv())
+    small_sum[...] = jnp.sum(small_recv[...], axis=0)
+
+    def small_line_copy(to_line, from_line, p):
+        return copy(
+            small_sum.at[to_line], small_line.at[from_line], sl_s.at[to_line],
+            sl_r.at[from_line], row_dev(p * PLANE + my_place),
+        )
+
+    each_line(lambda p: small_line_copy(p, my_line, p).start())
+    small_line[my_line] = small_sum[my_line]
+    lax.fori_loop(blocks // 2, blocks, field_block, 0)
     each_line(lambda p: line_copy(p, p, p).wait_recv())
-    done[my_line, my_place] = jnp.sum(line_recv[...], axis=0)
+    each_line(lambda p: small_line_copy(p, p, p).wait_recv())
+    done[my_line, my_place, 0:tiles] = jnp.sum(line_recv[...], axis=0)
+    done[my_line, my_place, tiles] = jnp.sum(small_line[...], axis=0)
 
     def up_copy(line, send, recv, p):
         return copy(
@@ -447,6 +479,7 @@
         each_place(lambda p: done_copy(line, my_place, p).wait_send())
     each_place(lambda p: small_copy(p, my_place, p, my_place, p).wait_send())
     each_line(lambda p: line_copy(p, my_line, p).wait_send())
+    each_line(lambda p: small_line_copy(p, my_line, p).wait_send())
     each_line(lambda p: up_copy(my_line, p, my_line, p).wait_send())
     each_var(lambda p: swap_copy(mine, p, mine, p).wait_send())
     each_var(lambda p: stat_copy(mine, p, mine, p).wait_send())
@@ -455,11 +488,16 @@
 
 
 def finish(
-    n_rows, tiles, bias_tiles, tok_in, field_in, done,
-    tok_out, field_out, weight_out, bias_out, query_out,
+    n_rows, tiles, bias_tiles, tok_in, field_in, done_in,
+    tok_out, field_out, weight_out, bias_out, query_out, done, sems,
 ):
-    tok_out[...] = tok_in[...]
-    field_out[...] = field_in[...]
+    done_load = pltpu.make_async_copy(done_in, done, sems.at[0])
+    tok_move = pltpu.make_async_copy(tok_in, tok_out, sems.at[1])
+    field_move = pltpu.make_async_copy(field_in, field_out, sems.at[2])
+    done_load.start()
+    tok_move.start()
+    field_move.start()
+    done_load.wait()
     across = D // LANE
     for number in range(n_rows * tiles):
         slot, tile = number // tiles, number % tiles
@@ -478,6 +516,8 @@
         for half in range(LANE // DH):
             head = lane * (LANE // DH) + half
             query_out[head : head + 1, :] = row[0:1, half * DH : (half + 1) * DH]
+    tok_move.wait()
+    field_move.wait()
 
 
 def local(
@@ -535,11 +575,13 @@
             pltpu.VMEM((PLANE, lines, tiles, SUB, LANE), F32),
             pltpu.VMEM((PLANE, lines, SUB, LANE), F32),
             pltpu.VMEM((PLANE, lines, SUB, LANE), F32),
-            pltpu.VMEM((lines, tiles + 1, SUB, LANE), F32),
-            pltpu.VMEM((lines, tiles + 1, SUB, LANE), F32),
+            pltpu.VMEM((lines, tiles, SUB, LANE), F32),
+            pltpu.VMEM((lines, tiles, SUB, LANE), F32),
+            pltpu.VMEM((lines, SUB, LANE), F32),
+            pltpu.VMEM((lines, SUB, LANE), F32),
         ]
         + [row_sem] * 2 + [var_sem] * 6 + [row_sem] * 2 + [var_sem] * 2
-        + [row_sem, dma((PLANE, lines))] + [dma((PLANE,))] * 2 + [dma((lines,))] * 4
+        + [row_sem, dma((PLANE, lines))] + [dma((PLANE,))] * 2 + [dma((lines,))] * 6
         + [dma((lines, PLANE))] * 2 + [dma((2,))],
         compiler_params=pltpu.CompilerParams(
             collective_id=0, has_side_effects=True, vmem_limit_bytes=56 * 1024 * 1024
@@ -564,9 +606,10 @@
             jax.ShapeDtypeStruct((var_local, D), F32),
             jax.ShapeDtypeStruct((H, DH), F32),
         ),
-        in_specs=[vmem] * 3,
-        out_specs=(vmem,) * 5,
-        compiler_params=pltpu.CompilerParams(vmem_limit_bytes=32 * 1024 * 1024),
+        in_specs=[pl.BlockSpec(memory_space=pl.ANY)] * 3,
+        out_specs=(pl.BlockSpec(memory_space=pl.ANY),) * 2 + (vmem,) * 3,
+        scratch_shapes=[pltpu.VMEM((lines, PLANE, tiles + 1, SUB, LANE), F32), dma((3,))],
+        compiler_params=pltpu.CompilerParams(vmem_limit_bytes=60 * 1024 * 1024),
         name="finish",
     )(tokens, field_grad, done)
     if depth != slot_depth:

time: 55.8 us -> 66.4 us (1.19)
  Pallas kernels: 50.6 us -> 64.1 us
  local copies, waits for them, and re-layouts: 4.3 us -> 1.39 us
    pallas_call x1, Pallas kernels: 0.95 us -> 13.8 us  [local(): pl.pallas_call(functools.partial(finish, n_rows, tiles, var_local // SUB...]
    unnamed x9 -> x3, local copies, waits for them, and re-layouts: 4.3 us -> 1.39 us
where the time goes in v3:
time: 66.4 us; the launch traced here: 66.1 us
  Pallas kernels  64.1 us (97%)
  local copies, waits for them, and re-layouts  1.39 us (2%)
    pallas_call x1, Pallas kernels, local(): pl.pallas_call(functools.partial(kernel, n_rows, n_vars, var_local, block...  50.3 us
    pallas_call x1, Pallas kernels, local(): pl.pallas_call(functools.partial(finish, n_rows, tiles, var_local // SUB...  13.8 us
    unnamed x3, local copies, waits for them, and re-layouts  1.39 us

profile of v3, /device:TPU:0, one launch (start us, length us, event | category | flops | bytes accessed | tf_op | source)
XLA Modules:
  0.0 66.1 jit_solution(1341102536881414797)
XLA Ops:
  0.6 0.0 copy-start
  0.6 0.6 copy-done
  1.3 0.7 %copy.13.owner_col = s32[128,1]{1,0:T(8,128)} copy(s32[128,1]{0,1:T(1,128)S(1)} %copy-done) | data formatting | bytes 1024 | tf_op args[3]
  2.0 50.3 %encoder.1 = (bf16[256,512]{1,0:T(8,128)(2,1)}, f32[8,4096]{1,0:T(8,128)}, f32[4,4,9,8,128]{4,3,2,1,0:T(8,128)}) custom-call(bf16[8,4096]{1,0:T(8,128)(2,1)} %fields.1, s32[4,2048]{1,0:T(4,128)} %bitcast.6, f32[4,2048]{1,0:T(4,128)} %bitcast.7, s32[128,1]{1,0:T(8,128)} %copy.13.owner_col, s32[1,128]{1,0:T(1,128)} %bitcast.8, bf16[128,1024]{1,0:T(8,128)(2,1)} %bitcast.5, ...), custom_call_target="tpu_custom_call" | custom-call | tf_op jit(solution)/shard_map/encoder/pallas_call | solution.py:550
  52.3 13.8 %finish.1 = (bf16[256,512]{1,0:T(8,128)(2,1)}, f32[8,4096]{1,0:T(8,128)}, f32[128,1024]{1,0:T(8,128)}, f32[8,1024]{1,0:T(8,128)}, f32[16,64]{1,0:T(8,128)}) custom-call(bf16[256,512]{1,0:T(8,128)(2,1)} %get-tuple-element.13.tok_in, f32[8,4096]{1,0:T(8,128)} %get-tuple-element.14.field_in, f32[4,4,9,8,128]{4,3,2,1,0:T(8,128)} %get-tuple-element.15.done_in), custom_call_target="tpu_custom_call" | custom-call | tf_op jit(solution)/shard_map/finish/pallas_call | solution.py:601
Async XLA Ops:
  0.6 0.7 copy-start
